TPU v7x, 512 devices: a whole 4x8x8 slice. The times are simulated.
512 devices in a mesh: section: 8 (over z_hi, core), vocab: 64 (over z_lo, y, x).
Axes of the slice: x: 4, y: 8, z: 8 (z_hi: 4, z_lo: 2; z = z_hi * 2 + z_lo), core: 2. Of those that a mesh axis runs over, the one named last changes fastest.
Arguments:
- tap_hidden: bfloat16 [3, 320, 8192], P(None, 'section', 'vocab'), may hold values from -6 to 6
- join_weight: bfloat16 [3, 8192, 8192], P(None, 'vocab', 'section'), may hold values from -0.0390625 to 0.0390625
- norm_gain: float32 [8192], P('section'), may hold values from 0.1 to 1.9
- head_weight: bfloat16 [8192, 65536], P('section', 'vocab')
- target_logits: bfloat16 [320, 65536], P('section', 'vocab')
- seq_lengths: int32 [10], replicated, may hold values from 1 to 32, as said below
- seq_mask: int32 [10], replicated, may hold values 0 or 1
Outputs:
- draft_loss: float32 [], replicated
- join_grad: float32 [3, 8192, 8192], P(None, 'vocab', 'section')
- gain_grad: float32 [8192], P('section')
Inputs may be any that keep to these rules, and one draw needn't show every extreme that they name: `seq_lengths`: one rollout of the window is live at all its 32 positions.
All inputs are finite; a program needn't handle non-finite values.
Results may differ from a plain program's by a relative error of at most 0.0059.
Values may be sent and summed in bfloat16 or wider, within the bound.
A program may use at most 64 MiB of HBM per device.

v0:
```python
import jax
import jax.numpy as jnp
from jax import lax
from jax.sharding import PartitionSpec as P

SPAN = 32


LOSS_SCALE = 1024.0
EPS = 1e-05


def token_weights(first_row, row_total, seq_lengths, seq_mask):
    position = first_row + jnp.arange(row_total, dtype=jnp.int32)
    sequence = position // SPAN
    offset = position % SPAN
    seq_count = seq_lengths.shape[0]
    picked = sequence[:, None] == jnp.arange(seq_count, dtype=jnp.int32)[None, :]
    length = jnp.sum(jnp.where(picked, seq_lengths[None, :], 0), axis=1)
    keep = jnp.sum(jnp.where(picked, seq_mask[None, :], 0), axis=1)
    return jnp.where(
        offset < length, keep.astype(jnp.float32) / (length.astype(jnp.float32) * seq_count), 0.0
    )


def shards(tap_hidden, join_weight, norm_gain, head_weight, target_logits, seq_lengths, seq_mask):
    width_all = norm_gain.shape[0] * lax.axis_size("section")
    gathered = lax.all_gather(tap_hidden, "section", axis=1, tiled=True)
    block = gathered
    joined_part = lax.psum_scatter(
        jnp.einsum("ktf,kfd->td", block, join_weight, preferred_element_type=jnp.float32),
        "vocab",
        scatter_dimension=0,
        tiled=True,
    )
    square_sum = lax.psum(jnp.sum(joined_part * joined_part, axis=1), "section")
    inverse = lax.rsqrt(square_sum / width_all + EPS)[:, None]
    normed_part = (joined_part * inverse * norm_gain[None, :]).astype(jnp.bfloat16)
    normed_all = lax.all_gather(normed_part, "vocab", axis=0, tiled=True)
    partial_logits = jnp.dot(normed_all, head_weight, preferred_element_type=jnp.float32)
    draft = lax.psum(partial_logits, "section")
    target = lax.all_gather(target_logits, "section", axis=0, tiled=True).astype(jnp.float32)
    first_row = 0
    row_total = draft.shape[0]
    draft_top = jnp.max(draft, axis=1)
    target_top = jnp.max(target, axis=1)
    draft_peak, target_peak = lax.pmax((draft_top, target_top), "vocab")
    target_scaled = jnp.exp(target - target_peak[:, None])
    draft_sum, target_sum, cross = lax.psum(
        (
            jnp.sum(jnp.exp(draft - draft_peak[:, None]), axis=1),
            jnp.sum(target_scaled, axis=1),
            jnp.sum(target_scaled * (target - draft), axis=1),
        ),
        "vocab",
    )
    draft_lse = draft_peak + jnp.log(draft_sum)
    target_lse = target_peak + jnp.log(target_sum)
    divergence = cross / target_sum - target_lse + draft_lse
    weight = token_weights(first_row, row_total, seq_lengths, seq_mask)
    partial_loss = jnp.sum(weight * divergence)
    target_prob = jnp.exp(target - target_peak[:, None]) / target_sum[:, None]
    dlogit = (
        LOSS_SCALE * weight[:, None] * (jnp.exp(draft - draft_lse[:, None]) - target_prob)
    ).astype(jnp.bfloat16)
    block = dlogit
    dnormed = lax.psum_scatter(
        lax.dot_general(
            block, head_weight, (((1,), (1,)), ((), ())), preferred_element_type=jnp.float32
        ),
        "vocab",
        scatter_dimension=0,
        tiled=True,
    )
    scaled = dnormed * norm_gain[None, :]
    inner = lax.psum(jnp.sum(scaled * joined_part, axis=1), "section")[:, None]
    gain_grad = lax.psum(jnp.sum(dnormed * joined_part * inverse, axis=0), "vocab")
    dfused = (scaled * inverse - joined_part * inner * inverse**3 / width_all).astype(jnp.bfloat16)
    block = gathered
    join_grad = jnp.einsum(
        "ktf,td->kfd",
        block,
        lax.all_gather(dfused, "vocab", axis=0, tiled=True),
        preferred_element_type=jnp.float32,
    )
    return (partial_loss, join_grad, gain_grad)


def solution(mesh):
    in_specs = (
        P(None, "section", "vocab"),
        P(None, "vocab", "section"),
        P("section"),
        P("section", "vocab"),
        P("section", "vocab"),
        P(),
        P(),
    )
    out_specs = (P(), P(None, "vocab", "section"), P("section"))
    return jax.shard_map(shards, mesh=mesh, in_specs=in_specs, out_specs=out_specs, check_vma=False)
```

profile of v0, /device:TPU:1, one launch (start us, length us, event | category | flops | bytes accessed | tf_op | source)
XLA Modules:
  0.0 2107.0 jit_solution(14500342460714564126)
XLA Ops:
  7.2 0.0 copy-start
  7.2 0.0 all-reduce.11.cloned.1.call-start
  7.2 22.0 %all_gather.13 = bf16[3,320,128]{2,1,0:T(8,128)(2,1)S(1)} all-gather(bf16[3,40,128]{2,1,0:T(8,128)(2,1)} %param.7), channel_id=1, replica_groups=mesh['section'=8,'vocab'=64] {'section'}, dimensions={1}, use_global_device_ids=true | all-gather | bytes 276480 | tf_op jit(solution)/shard_map/all_gather | solution.py:28
  29.2 0.0 copy-start.2
  29.2 2.7 convolution_bitcast_fusion.1
  31.9 0.0 all-reduce.11.cloned.1.call-update
  31.9 0.0 all-reduce.9.cloned.1.call-start
  32.0 1.3 dynamic-slice
  33.9 555.0 %all-reduce.11.cloned.1.call-done = f32[320,1024]{1,0:T(8,128)} async-done(((f32[320,1024]{1,0:T(8,128)}), f32[320,1024]{1,0:T(8,128)}) %all-reduce.11.cloned.1.call-update) | async-done | bytes 1310736
  589.0 1.0 multiply_reduce_fusion.2
  589.9 53.4 %psum.49 = f32[5]{0:T(128)S(1)} all-reduce(f32[5]{0:T(128)S(1)} %multiply_reduce_fusion.2), channel_id=1, replica_groups=mesh['section'=8,'vocab'=64] {'section'}, use_global_device_ids=true, to_apply=%region_6.0 | all-reduce | flops 5 | bytes 40 | tf_op jit(solution)/shard_map/psum | solution.py:36
  643.4 0.0 copy-done.2
  643.4 0.9 fusion.10
  644.3 129.6 %all-gather = bf16[64,5,1024]{2,1,0:T(8,128)(2,1)S(1)} all-gather(bf16[1,5,1024]{2,1,0:T(8,128)(2,1)S(1)} %fusion.10), channel_id=1, replica_groups=mesh['section'=8,'vocab'=64] {'vocab'}, dimensions={0}, use_global_device_ids=true | all-gather | bytes 665600 | tf_op jit(solution)/shard_map/all_gather | solution.py:39
  773.9 1.1 reshape.53
  775.0 0.0 copy-done
  775.0 3.0 fusion.19
  778.0 0.0 copy-start.1
  778.0 0.0 copy-start.3
  778.0 0.0 copy-start.4
  778.0 0.0 all-reduce.9.cloned.1.call-update
  778.1 0.0 all-reduce.13.cloned.1.call-start
  778.1 0.8 copy-done.1
  778.9 47.0 %all_gather.12 = bf16[320,1024]{1,0:T(8,128)(2,1)S(1)} all-gather(bf16[40,1024]{1,0:T(8,128)(2,1)S(1)} %copy-done.1), channel_id=1, replica_groups=mesh['section'=8,'vocab'=64] {'section'}, dimensions={0}, use_global_device_ids=true | all-gather | bytes 737280 | tf_op jit(solution)/shard_map/all_gather | solution.py:42
  826.0 0.2 reduce_max.23
  826.1 0.0 copy-done.3
  826.1 0.0 copy-done.4
  826.1 0.1 select_reduce_fusion
  826.2 57.3 %all-reduce.9.cloned.1.call-done = f32[320,1024]{1,0:T(8,128)} async-done(((f32[320,1024]{1,0:T(8,128)}), f32[320,1024]{1,0:T(8,128)}) %all-reduce.9.cloned.1.call-update) | async-done | bytes 1310736 | tf_op jit(solution)/shard_map/psum | solution.py:41
  883.5 1.5 reduce_max.25
  885.0 129.8 %all-reduce.4 = (f32[320]{0:T(512)S(1)}, f32[320]{0:T(512)S(1)}) all-reduce(f32[320]{0:T(512)S(1)} %reduce_max.25, bf16[320]{0:T(512)(128)(2,1)S(1)} %reduce_max.23), channel_id=1, replica_groups=mesh['section'=8,'vocab'=64] {'vocab'}, use_global_device_ids=true, to_apply=%region_13.0 | all-reduce | flops 640 | bytes 4480 | tf_op jit(solution)/shard_map/pmax | solution.py:47
  1014.8 2.1 fusion.4
  1016.9 125.0 %all-reduce.3 = (f32[320]{0:T(512)S(1)}, f32[320]{0:T(512)S(1)}) all-reduce(f32[320]{0:T(512)S(1)} %get-tuple-element.18, f32[320]{0:T(512)S(1)} %get-tuple-element.19), channel_id=1, replica_groups=mesh['section'=8,'vocab'=64] {'vocab'}, use_global_device_ids=true, to_apply=%region_15.16 | all-reduce | flops 640 | bytes 5120 | tf_op jit(solution)/shard_map/psum | solution.py:49
  1141.9 3.5 fusion.8
  1145.5 0.0 all-reduce.13.cloned.1.call-update
  1145.5 606.6 %all-reduce.13.cloned.1.call-done = f32[320,1024]{1,0:T(8,128)} async-done(((f32[320,1024]{1,0:T(8,128)}), f32[320,1024]{1,0:T(8,128)}) %all-reduce.13.cloned.1.call-update) | async-done | bytes 1310736
  1752.1 1.1 multiply_reduce_fusion
  1753.2 128.9 %all-reduce.2 = (f32[320]{0:T(512)S(1)}, f32[1024]{0:T(1024)}) all-reduce(f32[320]{0:T(512)S(1)} %get-tuple-element.17, f32[1024]{0:T(1024)S(1)} %get-tuple-element.15), channel_id=1, replica_groups=mesh['section'=8,'vocab'=64] {'vocab'}, use_global_device_ids=true, to_apply=%region_9.0 | all-reduce | flops 1344 | bytes 10752 | tf_op jit(solution)/shard_map/psum | solution.py:49
  1882.0 0.6 multiply_reduce_fusion.3
  1882.6 81.9 %psum.54 = f32[5]{0:T(128)S(1)} all-reduce(f32[5]{0:T(128)S(1)} %get-tuple-element.16), channel_id=1, replica_groups=mesh['section'=8,'vocab'=64] {'section'}, use_global_device_ids=true, to_apply=%region_19.20 | all-reduce | flops 5 | bytes 40 | tf_op jit(solution)/shard_map/psum | solution.py:76
  1964.6 0.9 fusion.11
  1965.5 127.9 %all-gather.1 = bf16[64,5,1024]{2,1,0:T(8,128)(2,1)S(1)} all-gather(bf16[1,5,1024]{2,1,0:T(8,128)(2,1)S(1)} %fusion.11), channel_id=1, replica_groups=mesh['section'=8,'vocab'=64] {'vocab'}, dimensions={0}, use_global_device_ids=true | all-gather | bytes 665600 | tf_op jit(solution)/shard_map/all_gather | solution.py:83
  2093.4 1.1 reshape.57
  2094.5 2.9 convolution_bitcast_fusion
  2097.4 3.0 copy.13
  (4 shorter events, 0.0 us)
Async XLA Ops:
  7.2 767.9 %copy-start = (bf16[1024,1024]{1,0:T(8,128)(2,1)S(1)}, bf16[1024,1024]{1,0:T(8,128)(2,1)}, u32[]{:S(2)}) copy-start(bf16[1024,1024]{1,0:T(8,128)(2,1)} %param.10) | copy-start | bytes 6291460
  7.2 581.8 %all-reduce.11.cloned.1.call-start = ((), (), s32[]{:S(2)}) async-start(), calls=%async_computation.1 | async-start | bytes 2621440
  29.2 614.2 %copy-start.2 = (f32[1024]{0:T(1024)S(1)}, f32[1024]{0:T(1024)}, u32[]{:S(2)}) copy-start(f32[1024]{0:T(1024)} %param.9) | copy-start | bytes 12292
  31.9 851.6 %all-reduce.9.cloned.1.call-start = ((), (), s32[]{:S(2)}) async-start(), calls=%async_computation | async-start | bytes 2621440 | tf_op jit(solution)/shard_map/psum | solution.py:41
  778.0 0.9 copy-start.1
  778.0 48.1 %copy-start.3 = (s32[10]{0:T(128)S(1)}, s32[10]{0:T(128)}, u32[]{:S(2)}) copy-start(s32[10]{0:T(128)} %param.13) | copy-start | bytes 124
  778.0 48.1 %copy-start.4 = (s32[10]{0:T(128)S(1)}, s32[10]{0:T(128)}, u32[]{:S(2)}) copy-start(s32[10]{0:T(128)} %param.12) | copy-start | bytes 124
  778.1 974.1 %all-reduce.13.cloned.1.call-start = ((), (), s32[]{:S(2)}) async-start(), calls=%async_computation.2 | async-start | bytes 2621440
Sparse Core Ops, SparseCore 0:
  32.1 556.8 all-reduce.10
  778.2 105.2 all-reduce.8
  1145.6 606.4 all-reduce.12
where the time goes:
time: 2130 us; the launch traced here: 2110 us
  waiting for transfers between devices  1220 us (57%)
  blocking collectives  846 us (40%)
    unnamed x5, waiting for transfers between devices  1160 us
    psum x2, blocking collectives, shards(): lax.psum((jnp.sum(jnp.exp(draft - draft_peak[:, None]), axis=1), jnp.sum(...  254 us
    pmax x1, blocking collectives, shards(): draft_peak, target_peak = lax.pmax((draft_top, target_top), 'vocab')  130 us
    all_gather x1, blocking collectives, shards(): normed_all = lax.all_gather(normed_part, 'vocab', axis=0, tiled=True)  130 us
    all_gather x1, blocking collectives, shards(): lax.all_gather(dfused, 'vocab', axis=0, tiled=True)  128 us
    psum x1, blocking collectives, shards(): inner = lax.psum(jnp.sum(scaled * joined_part, axis=1), 'section')[:, None]  81.9 us
    psum x1, waiting for transfers between devices, shards(): draft = lax.psum(partial_logits, 'section')  57.3 us
    psum x1, blocking collectives, shards(): square_sum = lax.psum(jnp.sum(joined_part * joined_part, axis=1), 'section')  53.4 us
  transfers between devices with their start and end apart: 3, of which 3 were waited for; matrix products, arithmetic and copies ran while one was open for 0% of the time, Pallas kernels for 0%

commit v1 on v0

v1 whole, which is shorter than its diff:
```python
import jax
import jax.numpy as jnp
from jax import lax
from jax.experimental import pallas as pl
from jax.experimental.pallas import tpu as pltpu
from jax.sharding import PartitionSpec as P

MESH = pl.DeviceIdType.MESH
F32 = jnp.float32
BF16 = jnp.bfloat16

SPAN = 32
SEQS = 10
LOSS_SCALE = 1024.0
EPS = 1e-05
WIDTH = 8192
TAPS = 3
BLK = 40
TOK = 320
COL = 128
LOC = 1024


def fold(a):
    return jnp.concatenate([a[:, : LOC // 2], a[:, LOC // 2 :]], axis=0)


def unfold(a):
    return jnp.concatenate([a[:BLK], a[BLK:]], axis=1)


LEVELS = 32767.0
BOUND = TAPS * COL * 6.0 * 0.0390625


def pack(low, high):
    low = jnp.where(low < 0, low - 0.5, low + 0.5).astype(jnp.int32)
    high = jnp.where(high < 0, high - 0.5, high + 0.5).astype(jnp.int32)
    return (high << 16) | (low & 0xFFFF)


def unpack(word):
    return ((word << 16) >> 16).astype(F32), (word >> 16).astype(F32)


def root_code(a):
    root = jnp.sqrt(jnp.sqrt(jnp.minimum(jnp.abs(a) * (1.0 / BOUND), 1.0))) * LEVELS
    return jnp.where(a < 0, -root, root)


def root_value(code):
    code = code * (1.0 / LEVELS)
    return BOUND * (code * code) * (code * jnp.abs(code))


def both(a):
    return jnp.concatenate([a, a], axis=0)


def columns_to_rows(columns):
    lane = lax.broadcasted_iota(jnp.int32, (BLK, 128), 1)
    out = jnp.zeros((BLK, 128), F32)
    for i, column in enumerate(columns):
        out = jnp.where(lane == i, column, out)
    out = jnp.concatenate([out, jnp.zeros((128 - BLK, 128), F32)], axis=0)
    return out.T[:8]


def stack_rows(rows):
    sub = lax.broadcasted_iota(jnp.int32, (8, 128), 0)
    out = jnp.zeros((8, 128), F32)
    for i, row in enumerate(rows):
        out = jnp.where(sub == i, row, out)
    return out


def rows_to_columns(rows):
    return jnp.concatenate([rows, jnp.zeros((120, 128), F32)], axis=0).T


def merge_stats(parts):
    top_d, top_t = parts[0][0:1], parts[0][3:4]
    for p in parts[1:]:
        top_d = jnp.maximum(top_d, p[0:1])
        top_t = jnp.maximum(top_t, p[3:4])
    sums = [jnp.zeros((1, 128), F32) for _ in range(5)]
    for p in parts:
        a = jnp.exp(p[0:1] - top_d)
        b = jnp.exp(p[3:4] - top_t)
        sums[0] += a * p[1:2]
        sums[1] += a * p[2:3]
        sums[2] += b * p[4:5]
        sums[3] += b * p[5:6]
        sums[4] += b * p[6:7]
    return [top_d, sums[0], sums[1], top_t, sums[2], sums[3], sums[4]]


def kernel(
    tap_ref, jw_ref, gain_ref, head_ref, tl_ref, len_ref, mask_ref,
    loss_ref, jg_ref, gg_ref,
    tapg, tapl, sb1, rb1, a1, b1, p1, jy, sqx, ub, ul, cs, cr, ds, own, zs, zr, zss, zsr, sqb, invc,
    st0, st1, st2, dlb, dl, qb, sb2, rb2, a2, b2, p2, dn, df, ggb, dfl,
    s_tap, r_tap, s_x1, r_x1, s_y1, r_y1, s_g1, r_g1, s_sx, r_sx, s_u, r_u, s_c, r_c, s_z, r_z, s_zs, r_zs,
    s_sq, r_sq,
    s_s1, r_s1, s_s2, r_s2, s_dl, r_dl, s_fw, s_q, r_q, s_x2, r_x2, s_y2, r_y2, s_g2, r_g2,
    s_df, r_df, s_gg, r_gg,
):
    sec = lax.axis_index("section")
    voc = lax.axis_index("vocab")
    zh, c = lax.div(sec, 2), lax.rem(sec, 2)
    zl, y, x = lax.div(voc, 32), lax.rem(lax.div(voc, 4), 8), lax.rem(voc, 4)
    j = zl * 4 + x
    pi = c * 4 + zh

    sec_peers = []
    for a, b in ((2, 0), (2, 1), (1, 0), (3, 0), (1, 1), (3, 1), (0, 1)):
        zh2, c2 = lax.rem(zh + a, 4), lax.rem(c + b, 2)
        sec_peers.append((c2 * 4 + zh2, (zh2 * 2 + c2, voc)))
    zh_peers = []
    for a in (2, 1, 3):
        zh2 = lax.rem(zh + a, 4)
        zh_peers.append((zh2, (zh2 * 2 + c, voc)))
    core_dev = (zh * 2 + (1 - c), voc)
    xz_peers = []
    for a, b in ((1, 2), (1, 1), (1, 3), (0, 2), (0, 1), (0, 3), (1, 0)):
        zl2, x2 = lax.rem(zl + a, 2), lax.rem(x + b, 4)
        xz_peers.append((zl2 * 4 + x2, (sec, zl2 * 32 + y * 4 + x2)))
    y_peers = []
    for a in (4, 3, 5, 2, 6, 1, 7):
        y2 = lax.rem(y + a, 8)
        y_peers.append((y2, (sec, zl * 32 + y2 * 4 + x)))

    barrier = pltpu.get_barrier_semaphore()
    for _, dev in sec_peers + xz_peers + y_peers:
        pl.semaphore_signal(barrier, inc=1, device_id=dev, device_id_type=MESH)
    pl.semaphore_wait(barrier, 21)

    pending = []

    def send(src, dst, s_sem, r_sem, dev):
        copy = pltpu.make_async_remote_copy(src, dst, s_sem, r_sem, device_id=dev, device_id_type=MESH)
        copy.start()
        pending.append(copy)

    def send_all(peers, src, dst, s_sem, r_sem, slot):
        for k, (other, dev) in enumerate(peers):
            send(src(other), dst.at[slot], s_sem.at[k], r_sem.at[slot], dev)

    def arrived(dst, s_sem, r_sem, dev):
        pltpu.make_async_remote_copy(dst, dst, s_sem, r_sem, device_id=dev, device_id_type=MESH).wait_recv()

    def wait_all(peers, dst, s_sem, r_sem):
        for k, (other, dev) in enumerate(peers):
            arrived(dst.at[other], s_sem.at[k], r_sem.at[other], dev)

    send_all(sec_peers, lambda other: tap_ref, tapg, s_tap, r_tap, pi)
    tapg[pi] = tap_ref[...]
    wait_all(sec_peers, tapg, s_tap, r_tap)
    blocks = [tapg[p].astype(F32) for p in range(8)]
    for k in range(TAPS):
        rows = jnp.concatenate([b[k * BLK : (k + 1) * BLK] for b in blocks], axis=0)
        tapl[:, k * COL : (k + 1) * COL] = rows.astype(BF16)

    def join_step(i, carry):
        at = pl.ds(pl.multiple_of(i * 256, 256), 256)
        acc = jnp.dot(tapl[...], jw_ref[:, at], preferred_element_type=F32)
        acc = root_code(acc)
        sb1[2 * i] = pack(acc[:160, :COL], acc[160:, :COL])
        sb1[2 * i + 1] = pack(acc[:160, COL:], acc[160:, COL:])
        return carry

    lax.fori_loop(0, 4, join_step, 0)

    def from_roots(rb):
        low, high = [root_value(half) for half in unpack(rb[0])]
        for k in range(1, 8):
            more = [root_value(half) for half in unpack(rb[k])]
            low, high = low + more[0], high + more[1]
        return jnp.concatenate([low, high], axis=0)

    def from_bf16(rb):
        total = rb[0].astype(F32)
        for k in range(1, 8):
            total += rb[k].astype(F32)
        return total

    def vocab_sum(collect, sb, rb, a_buf, b_buf, p_buf, out, s_x, r_x, s_y, r_y, s_g, r_g):
        send_all(xz_peers, lambda other: sb.at[other], rb, s_x, r_x, j)
        rb[j] = sb[j]
        wait_all(xz_peers, rb, s_x, r_x)
        total = collect(rb)
        for k in range(8):
            a_buf[k] = total[k * BLK : (k + 1) * BLK]
        send_all(y_peers, lambda other: a_buf.at[other], b_buf, s_y, r_y, y)
        b_buf[y] = a_buf[y]
        wait_all(y_peers, b_buf, s_y, r_y)
        piece = b_buf[0]
        for k in range(1, 8):
            piece += b_buf[k]
        p_buf[...] = piece
        send_all(y_peers, lambda other: p_buf, out, s_g, r_g, y)
        out[y] = piece
        wait_all(y_peers, out, s_g, r_g)

    vocab_sum(from_roots, sb1, rb1, a1, b1, p1, jy, s_x1, r_x1, s_y1, r_y1, s_g1, r_g1)

    joined = jnp.concatenate([jy[k] for k in range(8)], axis=0)
    square = jnp.concatenate([joined * joined, jnp.zeros((64, COL), F32)], axis=0)
    sqx[j] = jnp.sum(square.T, axis=0, keepdims=True)
    send_all(xz_peers, lambda other: sqx.at[j], sqx, s_sx, r_sx, j)
    code = joined * (LEVELS * lax.rsqrt(jnp.maximum(jnp.sum(square[:TOK], axis=1, keepdims=True), 1e-30)))
    ub[j] = pack(code[:160], code[160:])
    send_all(xz_peers, lambda other: ub.at[j], ub, s_u, r_u, j)
    wait_all(xz_peers, sqx, s_sx, r_sx)
    square = sqx[0]
    for k in range(1, 8):
        square += sqx[k]
    sqb[pi] = square
    send_all(sec_peers, lambda other: sqb.at[pi], sqb, s_sq, r_sq, pi)
    wait_all(sec_peers, sqb, s_sq, r_sq)
    square = sqb[0]
    for k in range(1, 8):
        square += sqb[k]
    inverse = lax.rsqrt(square / WIDTH + EPS)
    factors = [jnp.sqrt(sqx[k]) * (1.0 / LEVELS) * inverse for k in range(8)]
    factors = jnp.concatenate(factors + [jnp.zeros((120, 384), F32)], axis=0).T
    inverse = jnp.broadcast_to(inverse, (128, 384)).T
    for k in range(8):
        invc[k] = inverse[k * BLK : (k + 1) * BLK]
    wait_all(xz_peers, ub, s_u, r_u)
    for k in range(8):
        for h, half in enumerate(unpack(ub[k])):
            normed = half * factors[h * 160 : (h + 1) * 160, k : k + 1] * gain_ref[k : k + 1, :]
            ul[h, :, k * COL : (k + 1) * COL] = normed.astype(BF16)

    def draft_half(half, out):
        def step(i, carry):
            at = pl.ds(pl.multiple_of(i * 256, 256), 256)
            out[:, at] = jnp.dot(ul[half], head_ref[:, at], preferred_element_type=F32)
            return carry

        lax.fori_loop(0, 4, step, 0)

    draft_half(1 - c, cs)
    send(cs, cr, s_c, r_c, core_dev)

    draft_half(c, ds)
    arrived(cr, s_c, r_c, core_dev)
    tops = []
    for k in range(4):
        rows = slice(k * BLK, (k + 1) * BLK)
        part = ds[rows, :] + cr[rows, :]
        ds[rows, :] = part
        tops.append(jnp.maximum(jnp.max(jnp.abs(part), axis=1, keepdims=True), 1e-30))
        code = part * (LEVELS / tops[-1])
        zs[k] = pack(code[:, : LOC // 2], code[:, LOC // 2 :])
    zss[...] = columns_to_rows(tops)
    for k, (other, dev) in enumerate(zh_peers):
        send(zss, zsr.at[zh], s_zs.at[k], r_zs.at[zh], dev)
        send(zs.at[other], zr.at[zh], s_z.at[k], r_z.at[zh], dev)
    zsr[zh] = zss[...]
    own[...] = fold(ds[pl.ds(pl.multiple_of(zh * BLK, 8), BLK), :])
    target = fold(tl_ref[...].astype(F32))

    lane = lax.broadcasted_iota(jnp.int32, (1, 128), 1)
    position = sec * BLK + lane
    sequence = position // SPAN
    offset = position % SPAN
    length = jnp.zeros((1, 128), jnp.int32)
    keep = jnp.zeros((1, 128), jnp.int32)
    for q in range(SEQS):
        length = jnp.where(sequence == q, len_ref[q], length)
        keep = jnp.where(sequence == q, mask_ref[q], keep)
    live = (offset < length) & (lane < BLK)
    weight = jnp.where(live, keep.astype(F32) / (jnp.maximum(length, 1).astype(F32) * SEQS), 0.0)

    wait_all(zh_peers, zsr, s_zs, r_zs)
    steps = rows_to_columns(stack_rows([zsr[other, pl.ds(zh, 1), :] for other, _ in zh_peers])) * (1.0 / LEVELS)
    draft = own[...]
    for k, (other, dev) in enumerate(zh_peers):
        arrived(zr.at[other], s_z.at[k], r_z.at[other], dev)
        draft += jnp.concatenate(unpack(zr[other]), axis=0) * both(steps[:BLK, k : k + 1])

    def per_token(a, op, reduce):
        m = op(op(a[:, :128], a[:, 128:256]), op(a[:, 256:384], a[:, 384:]))
        return reduce(op(m[:BLK], m[BLK:]), axis=1, keepdims=True)

    def top(a):
        return per_token(a, jnp.maximum, jnp.max)

    def add(a):
        return per_token(a, jnp.add, jnp.sum)

    d_top = top(draft)
    d_exp = jnp.exp(draft - both(d_top))
    t_top = top(target)
    t_exp = jnp.exp(target - both(t_top))
    st0[...] = columns_to_rows(
        [d_top, add(d_exp), add(d_exp * draft), t_top, add(t_exp), add(t_exp * (target - draft)), add(t_exp * draft)]
    )
    send_all(xz_peers, lambda other: st0, st1, s_s1, r_s1, j)
    st1[j] = st0[...]
    wait_all(xz_peers, st1, s_s1, r_s1)
    st2[y] = stack_rows(merge_stats([st1[k] for k in range(8)]))
    send_all(y_peers, lambda other: st2.at[y], st2, s_s2, r_s2, y)
    wait_all(y_peers, st2, s_s2, r_s2)
    d_top, d_sum, d_first, t_top, t_sum, cross, t_first = merge_stats([st2[k] for k in range(8)])
    valid = lane < BLK
    d_sum = jnp.where(valid, d_sum, 1.0)
    t_sum = jnp.where(valid, t_sum, 1.0)
    d_lse = d_top + jnp.log(d_sum)
    t_lse = t_top + jnp.log(t_sum)
    loss = weight * (cross / t_sum - t_lse + d_lse)
    scale = LOSS_SCALE * weight
    along = scale * (d_first / d_sum - t_first / t_sum)

    cols = rows_to_columns(stack_rows([d_lse, scale, t_top, scale / t_sum]))
    dlogit = both(cols[:BLK, 1:2]) * jnp.exp(draft - both(cols[:BLK, 0:1])) - both(cols[:BLK, 3:4]) * jnp.exp(
        target - both(cols[:BLK, 2:3])
    )
    dlb[pi] = dlogit.astype(BF16)
    for k, (other, dev) in enumerate(zh_peers):
        send(dlb.at[pi], dlb.at[pi], s_dl.at[k], r_dl.at[pi], dev)
    send(dlb.at[pi], dlb.at[pi], s_fw.at[3], r_dl.at[pi], core_dev)
    qb[pi] = stack_rows([along, loss])
    send_all(sec_peers, lambda other: qb.at[pi], qb, s_q, r_q, pi)
    for k, (other, dev) in enumerate(zh_peers[1:] + zh_peers[:1]):
        slot = c * 4 + other
        arrived(dlb.at[slot], s_dl.at[k], r_dl.at[slot], dev)
        send(dlb.at[slot], dlb.at[slot], s_fw.at[k], r_dl.at[slot], core_dev)

    def grad_half(half):
        for k in range(0, 4, 2):
            pair = [unfold(dlb[half * 4 + k + i].astype(F32)) for i in range(2)]
            dl[half, k * BLK : (k + 2) * BLK] = jnp.concatenate(pair, axis=0).astype(BF16)

        def step(i, carry):
            at = pl.ds(pl.multiple_of(i * 256, 256), 256)
            acc = lax.dot_general(
                dl[half], head_ref[at, :], (((1,), (1,)), ((), ())), preferred_element_type=F32
            )
            rows = pl.ds(pl.multiple_of(half * 160, 16), 160)
            sb2[2 * i, rows] = acc[:, :COL].astype(BF16)
            sb2[2 * i + 1, rows] = acc[:, COL:].astype(BF16)
            return carry

        lax.fori_loop(0, 4, step, 0)

    grad_half(c)
    for zh2 in range(4):
        slot = (1 - c) * 4 + zh2
        arrived(dlb.at[slot], s_fw.at[0], r_dl.at[slot], core_dev)
    grad_half(1 - c)

    vocab_sum(from_bf16, sb2, rb2, a2, b2, p2, dn, s_x2, r_x2, s_y2, r_y2, s_g2, r_g2)

    wait_all(sec_peers, qb, s_q, r_q)
    loss = qb[0, 1:2]
    for k in range(1, 8):
        loss += qb[k, 1:2]
    loss_ref[0, 0] = jnp.sum(loss)
    q_cols = rows_to_columns(stack_rows([qb[k, 0:1] for k in range(8)]))
    gain = gain_ref[pl.ds(j, 1), :]
    gg = jnp.zeros((BLK, COL), F32)
    pair = []
    for k in range(8):
        inv = invc[k]
        joined = jy[k]
        grad = dn[k] * inv
        gg += grad * joined
        pair.append(grad * gain - joined * (q_cols[:BLK, k : k + 1] * inv * inv / WIDTH))
        if k % 2:
            df[j, (k - 1) * BLK : (k + 1) * BLK] = jnp.concatenate(pair, axis=0).astype(BF16)
            pair = []
    send_all(xz_peers, lambda other: df.at[j], df, s_df, r_df, j)
    ggb[j] = jnp.sum(gg, axis=0, keepdims=True)
    send_all(xz_peers, lambda other: ggb.at[j], ggb, s_gg, r_gg, j)
    wait_all(xz_peers, df, s_df, r_df)
    for k in range(8):
        dfl[:, k * COL : (k + 1) * COL] = df[k]

    def out_step(i, carry):
        at = pl.ds(pl.multiple_of(i * 256, 256), 256)
        for k in range(TAPS):
            jg_ref[k * COL : (k + 1) * COL, at] = lax.dot_general(
                tapl[:, k * COL : (k + 1) * COL], dfl[:, at], (((0,), (0,)), ((), ())), preferred_element_type=F32
            )
        return carry

    lax.fori_loop(0, 4, out_step, 0)
    wait_all(xz_peers, ggb, s_gg, r_gg)
    for k in range(8):
        gg_ref[k : k + 1, :] = ggb[k]
    for copy in pending:
        copy.wait_send()


def shards(tap_hidden, join_weight, norm_gain, head_weight, target_logits, seq_lengths, seq_mask):
    taps = jnp.pad(tap_hidden.reshape(TAPS * BLK, COL), ((0, 128 - TAPS * BLK), (0, 0)))
    vmem = pl.BlockSpec(memory_space=pltpu.VMEM)
    smem = pl.BlockSpec(memory_space=pltpu.SMEM)
    dma = pltpu.SemaphoreType.DMA
    V = pltpu.VMEM
    scratch = [
        V((8, 128, COL), BF16), V((TOK, TAPS * COL), BF16),
        V((8, TOK // 2, COL), jnp.int32), V((8, TOK // 2, COL), jnp.int32),
        V((8, BLK, COL), F32), V((8, BLK, COL), F32), V((BLK, COL), F32), V((8, BLK, COL), F32),
        V((8, 1, 384), F32), V((8, TOK // 2, COL), jnp.int32), V((2, TOK // 2, LOC), BF16),
        V((TOK // 2, LOC), F32), V((TOK // 2, LOC), F32), V((TOK // 2, LOC), F32),
        V((2 * BLK, LOC // 2), F32),
        V((4, BLK, LOC // 2), jnp.int32), V((4, BLK, LOC // 2), jnp.int32), V((8, 128), F32), V((4, 8, 128), F32),
        V((8, 1, 384), F32), V((8, BLK, COL), F32),
        V((8, 128), F32), V((8, 8, 128), F32), V((8, 8, 128), F32),
        V((8, 2 * BLK, LOC // 2), BF16), V((2, TOK // 2, LOC), BF16), V((8, 8, 128), F32),
        V((8, TOK, COL), BF16), V((8, TOK, COL), BF16),
        V((8, BLK, COL), F32), V((8, BLK, COL), F32), V((BLK, COL), F32), V((8, BLK, COL), F32),
        V((8, TOK, COL), BF16), V((8, 1, COL), F32), V((TOK, LOC), BF16),
        dma((7,)), dma((8,)),
        dma((7,)), dma((8,)), dma((7,)), dma((8,)), dma((7,)), dma((8,)),
        dma((7,)), dma((8,)), dma((7,)), dma((8,)),
        dma, dma,
        dma((3,)), dma((4,)), dma((3,)), dma((4,)),
        dma((7,)), dma((8,)),
        dma((7,)), dma((8,)), dma((7,)), dma((8,)),
        dma((3,)), dma((8,)), dma((4,)),
        dma((7,)), dma((8,)),
        dma((7,)), dma((8,)), dma((7,)), dma((8,)), dma((7,)), dma((8,)),
        dma((7,)), dma((8,)), dma((7,)), dma((8,)),
    ]
    loss, join_grad, gain_grad = pl.pallas_call(
        kernel,
        out_shape=(
            jax.ShapeDtypeStruct((1, 1), F32),
            jax.ShapeDtypeStruct((TAPS * COL, LOC), F32),
            jax.ShapeDtypeStruct((8, COL), F32),
        ),
        in_specs=[vmem] * 5 + [smem] * 2,
        out_specs=(smem, vmem, vmem),
        scratch_shapes=scratch,
        compiler_params=pltpu.CompilerParams(
            collective_id=0, has_side_effects=True, vmem_limit_bytes=48 * 1024 * 1024
        ),
        name="draft_step",
    )(
        taps,
        join_weight.reshape(TAPS * COL, LOC),
        norm_gain.reshape(8, COL),
        head_weight,
        target_logits,
        seq_lengths,
        seq_mask,
    )
    return loss.reshape(()), join_grad.reshape(TAPS, COL, LOC), gain_grad.reshape(LOC)


def solution(mesh):
    in_specs = (
        P(None, "section", "vocab"),
        P(None, "vocab", "section"),
        P("section"),
        P("section", "vocab"),
        P("section", "vocab"),
        P(),
        P(),
    )
    out_specs = (P(), P(None, "vocab", "section"), P("section"))
    return jax.shard_map(shards, mesh=mesh, in_specs=in_specs, out_specs=out_specs, check_vma=False)
```

time: 2130 us -> 138 us (0.06); the launches traced: 2110 us -> 138 us
  waiting for transfers between devices: 1220 us -> 0 us
  blocking collectives: 846 us -> 0 us
  Pallas kernels: 0 us -> 128 us
    unnamed x5 -> x0, waiting for transfers between devices: 1160 us -> none
    psum x4 -> x0, blocking collectives: 389 us -> none  [the longest x2 254 us: shards(): lax.psum((jnp.sum(jnp.exp(draft - draft_peak[:, None]), axis=1), jnp.sum(...]
    all_gather x4 -> x0, blocking collectives: 327 us -> none  [the longest x1 130 us: shards(): normed_all = lax.all_gather(normed_part, 'vocab', axis=0, tiled=True)]
    pmax x1 -> x0, blocking collectives: 130 us -> none  [shards(): draft_peak, target_peak = lax.pmax((draft_top, target_top), 'vocab')]
    pallas_call x0 -> x1, Pallas kernels: none -> 128 us  [shards(): pl.pallas_call(kernel, out_shape=(jax.ShapeDtypeStruct((1, 1), F32), jax....]
    psum x1 -> x0, waiting for transfers between devices: 57.3 us -> none  [shards(): draft = lax.psum(partial_logits, 'section')]
  transfers between devices with their start and end apart: 3 -> 0, of which waited for: 3 -> 0; matrix products, arithmetic and copies ran while one was open for 0% -> 0% of each run, Pallas kernels for 0% -> 0%
where the time goes in v1:
time: 138 us
  Pallas kernels  128 us (93%)
  local copies, waits for them, and re-layouts  8.1 us (6%)
  between operations  2.46 us (2%)
    pallas_call x1, Pallas kernels, shards(): pl.pallas_call(kernel, out_shape=(jax.ShapeDtypeStruct((1, 1), F32), jax....  128 us
    unnamed x14, local copies, waits for them, and re-layouts  7.34 us

profile of v1, /device:TPU:1, one launch (start us, length us, event | category | flops | bytes accessed | tf_op | source)
XLA Modules:
  0.0 138.1 jit_solution(2255175221748613768)
XLA Ops:
  0.6 0.8 pad.4.tap_ref
  1.4 0.0 copy-start
  1.4 1.6 %copy-done = bf16[1024,1024]{1,0:T(8,128)(2,1)S(1)} copy-done((bf16[1024,1024]{1,0:T(8,128)(2,1)S(1)}, bf16[1024,1024]{1,0:T(8,128)(2,1)}, u32[]{:S(2)}) %copy-start) | copy-done | bytes 2097176
  3.0 0.0 copy-start.1
  3.0 1.1 copy-done.1
  4.1 0.0 copy-start.2
  4.1 0.9 copy-done.2
  5.0 0.0 copy-start.3
  5.0 0.7 copy-done.3
  5.7 0.0 copy-start.4
  5.7 0.7 copy-done.4
  6.3 0.0 copy-start.5
  6.3 0.7 copy-done.5
  7.0 127.6 %draft_step.1 = (f32[1,1]{1,0:T(1,128)}, f32[384,1024]{1,0:T(8,128)S(1)}, f32[8,128]{1,0:T(8,128)S(1)}) custom-call(bf16[128,128]{1,0:T(8,128)(2,1)S(1)} %pad.4.tap_ref, bf16[384,1024]{1,0:T(8,128)(2,1)S(1)} %bitcast.7, f32[8,128]{1,0:T(8,128)S(1)} %bitcast.8, bf16[1024,1024]{1,0:T(8,128)(2,1)S(1)} %copy-done, bf16[40,1024]{1,0:T(8,128)(2,1)S(1)} %copy-done.2, ...), custom_call_target="tpu_custom_call" | custom-call | tf_op jit(solution)/shard_map/draft_step/pallas_call | solution.py:430
  135.3 1.1 copy.14
  136.4 0.6 copy.15
Async XLA Ops:
  1.4 1.6 %copy-start = (bf16[1024,1024]{1,0:T(8,128)(2,1)S(1)}, bf16[1024,1024]{1,0:T(8,128)(2,1)}, u32[]{:S(2)}) copy-start(bf16[1024,1024]{1,0:T(8,128)(2,1)} %head_ref.1) | copy-start | bytes 6291460
  3.0 1.1 copy-start.1
  4.1 0.9 copy-start.2
  5.0 0.7 copy-start.3
  5.7 0.7 copy-start.4
  6.3 0.7 copy-start.5

commit v2 on v1

--- a/solution.py
+++ b/solution.py
@@ -96,11 +96,12 @@
 
 
 def kernel(
+    tap_hbm, jw_hbm, gain_hbm, head_hbm, tl_hbm, len_hbm, mask_hbm,
+    loss_ref, jg_ref, gg_ref,
     tap_ref, jw_ref, gain_ref, head_ref, tl_ref, len_ref, mask_ref,
-    loss_ref, jg_ref, gg_ref,
     tapg, tapl, sb1, rb1, a1, b1, p1, jy, sqx, ub, ul, cs, cr, ds, own, zs, zr, zss, zsr, sqb, invc,
     st0, st1, st2, dlb, dl, qb, sb2, rb2, a2, b2, p2, dn, df, ggb, dfl,
-    s_tap, r_tap, s_x1, r_x1, s_y1, r_y1, s_g1, r_g1, s_sx, r_sx, s_u, r_u, s_c, r_c, s_z, r_z, s_zs, r_zs,
+    s_in, s_tap, r_tap, s_tf, s_x1, r_x1, s_y1, r_y1, s_g1, r_g1, s_sx, r_sx, s_u, r_u, s_c, r_c, s_z, r_z, s_zs, r_zs,
     s_sq, r_sq,
     s_s1, r_s1, s_s2, r_s2, s_dl, r_dl, s_fw, s_q, r_q, s_x2, r_x2, s_y2, r_y2, s_g2, r_g2,
     s_df, r_df, s_gg, r_gg,
@@ -130,9 +131,20 @@
         y2 = lax.rem(y + a, 8)
         y_peers.append((y2, (sec, zl * 32 + y2 * 4 + x)))
 
+    inputs = (
+        (tap_hbm, tap_ref), (jw_hbm, jw_ref), (gain_hbm, gain_ref), (len_hbm, len_ref), (mask_hbm, mask_ref),
+        (head_hbm, head_ref), (tl_hbm, tl_ref),
+    )
+    loads = [pltpu.make_async_copy(src, dst, s_in.at[i]) for i, (src, dst) in enumerate(inputs)]
+    for load in loads:
+        load.start()
+
     barrier = pltpu.get_barrier_semaphore()
     for _, dev in sec_peers + xz_peers + y_peers:
         pl.semaphore_signal(barrier, inc=1, device_id=dev, device_id_type=MESH)
+    loads[0].wait()
+    taps = [tap_ref[k].astype(F32) for k in range(TAPS)] + [jnp.zeros((128 - TAPS * BLK, COL), F32)]
+    tapg[pi] = jnp.concatenate(taps, axis=0).astype(BF16)
     pl.semaphore_wait(barrier, 21)
 
     pending = []
@@ -153,9 +165,18 @@
         for k, (other, dev) in enumerate(peers):
             arrived(dst.at[other], s_sem.at[k], r_sem.at[other], dev)
 
-    send_all(sec_peers, lambda other: tap_ref, tapg, s_tap, r_tap, pi)
-    tapg[pi] = tap_ref[...]
-    wait_all(sec_peers, tapg, s_tap, r_tap)
+    for k, (other, dev) in enumerate(zh_peers):
+        send(tapg.at[pi], tapg.at[pi], s_tap.at[k], r_tap.at[pi], dev)
+    send(tapg.at[pi], tapg.at[pi], s_tf.at[3], r_tap.at[pi], core_dev)
+    for k, (other, dev) in enumerate(zh_peers[1:] + zh_peers[:1]):
+        slot = c * 4 + other
+        arrived(tapg.at[slot], s_tap.at[k], r_tap.at[slot], dev)
+        send(tapg.at[slot], tapg.at[slot], s_tf.at[k], r_tap.at[slot], core_dev)
+    for load in loads[1:]:
+        load.wait()
+    for zh2 in range(4):
+        slot = (1 - c) * 4 + zh2
+        arrived(tapg.at[slot], s_tf.at[0], r_tap.at[slot], core_dev)
     blocks = [tapg[p].astype(F32) for p in range(8)]
     for k in range(TAPS):
         rows = jnp.concatenate([b[k * BLK : (k + 1) * BLK] for b in blocks], axis=0)
@@ -396,12 +417,14 @@
 
 
 def shards(tap_hidden, join_weight, norm_gain, head_weight, target_logits, seq_lengths, seq_mask):
-    taps = jnp.pad(tap_hidden.reshape(TAPS * BLK, COL), ((0, 128 - TAPS * BLK), (0, 0)))
     vmem = pl.BlockSpec(memory_space=pltpu.VMEM)
     smem = pl.BlockSpec(memory_space=pltpu.SMEM)
     dma = pltpu.SemaphoreType.DMA
     V = pltpu.VMEM
+    hbm = pl.BlockSpec(memory_space=pl.ANY)
     scratch = [
+        V((TAPS, BLK, COL), BF16), V((TAPS * COL, LOC), BF16), V((8, COL), F32), V((LOC, LOC), BF16),
+        V((BLK, LOC), BF16), pltpu.SMEM((SEQS,), jnp.int32), pltpu.SMEM((SEQS,), jnp.int32),
         V((8, 128, COL), BF16), V((TOK, TAPS * COL), BF16),
         V((8, TOK // 2, COL), jnp.int32), V((8, TOK // 2, COL), jnp.int32),
         V((8, BLK, COL), F32), V((8, BLK, COL), F32), V((BLK, COL), F32), V((8, BLK, COL), F32),
@@ -415,7 +438,7 @@
         V((8, TOK, COL), BF16), V((8, TOK, COL), BF16),
         V((8, BLK, COL), F32), V((8, BLK, COL), F32), V((BLK, COL), F32), V((8, BLK, COL), F32),
         V((8, TOK, COL), BF16), V((8, 1, COL), F32), V((TOK, LOC), BF16),
-        dma((7,)), dma((8,)),
+        dma((7,)), dma((3,)), dma((8,)), dma((4,)),
         dma((7,)), dma((8,)), dma((7,)), dma((8,)), dma((7,)), dma((8,)),
         dma((7,)), dma((8,)), dma((7,)), dma((8,)),
         dma, dma,
@@ -434,15 +457,15 @@
             jax.ShapeDtypeStruct((TAPS * COL, LOC), F32),
             jax.ShapeDtypeStruct((8, COL), F32),
         ),
-        in_specs=[vmem] * 5 + [smem] * 2,
+        in_specs=[hbm] * 7,
         out_specs=(smem, vmem, vmem),
         scratch_shapes=scratch,
         compiler_params=pltpu.CompilerParams(
-            collective_id=0, has_side_effects=True, vmem_limit_bytes=48 * 1024 * 1024
+            collective_id=0, has_side_effects=True, vmem_limit_bytes=60 * 1024 * 1024
         ),
         name="draft_step",
     )(
-        taps,
+        tap_hidden,
         join_weight.reshape(TAPS * COL, LOC),
         norm_gain.reshape(8, COL),
         head_weight,

time: 138 us -> 133 us (0.964)
  local copies, waits for them, and re-layouts: 8.1 us -> 3.33 us
    unnamed x14 -> x4, local copies, waits for them, and re-layouts: 7.34 us -> 3.33 us
where the time goes in v2:
time: 133 us
  Pallas kernels  127 us (95%)
  local copies, waits for them, and re-layouts  3.33 us (3%)
  between operations  2.41 us (2%)
    pallas_call x1, Pallas kernels, shards(): pl.pallas_call(kernel, out_shape=(jax.ShapeDtypeStruct((1, 1), F32), jax....  127 us
    unnamed x4, local copies, waits for them, and re-layouts  3.33 us

profile of v2, /device:TPU:1, one launch (start us, length us, event | category | flops | bytes accessed | tf_op | source)
XLA Modules:
  0.0 132.8 jit_solution(8834407363892675315)
XLA Ops:
  0.6 127.0 %draft_step.1 = (f32[1,1]{1,0:T(1,128)}, f32[384,1024]{1,0:T(8,128)}, f32[8,128]{1,0:T(8,128)}) custom-call(bf16[3,40,128]{2,1,0:T(8,128)(2,1)} %tap_hbm.1, bf16[384,1024]{1,0:T(8,128)(2,1)} %bitcast.6, f32[8,128]{1,0:T(8,128)} %bitcast.7, bf16[1024,1024]{1,0:T(8,128)(2,1)} %head_hbm.1, bf16[40,1024]{1,0:T(8,128)(2,1)} %tl_hbm.1, s32[10]{0:T(128)} %len_hbm.1, ...), custom_call_target="tpu_custom_call" | custom-call | tf_op jit(solution)/shard_map/draft_step/pallas_call | solution.py:453
  128.3 0.0 copy-start
  128.3 2.7 %copy.14 = f32[3,128,1024]{2,1,0:T(8,128)} copy(f32[3,128,1024]{2,1,0:T(8,128)} %bitcast.5) | data formatting | bytes 3145728
  131.0 0.0 copy-done
  131.0 0.6 copy.15
Async XLA Ops:
  128.3 2.7 %copy-start = (f32[8,128]{1,0:T(8,128)S(1)}, f32[8,128]{1,0:T(8,128)}, u32[]{:S(2)}) copy-start(f32[8,128]{1,0:T(8,128)} %get-tuple-element.8) | copy-start | bytes 12292

commit v3 on v2

v3 whole, which is shorter than its diff:
```python
import jax
import jax.numpy as jnp
from jax import lax
from jax.experimental import pallas as pl
from jax.experimental.pallas import tpu as pltpu
from jax.sharding import PartitionSpec as P

MESH = pl.DeviceIdType.MESH
F32 = jnp.float32
BF16 = jnp.bfloat16

SPAN = 32
SEQS = 10
LOSS_SCALE = 1024.0
EPS = 1e-05
WIDTH = 8192
TAPS = 3
BLK = 40
SPLITS = (16, 16, 8)
TOK = 320
COL = 128
LOC = 1024


def fold(a):
    return jnp.concatenate([a[:, : LOC // 2], a[:, LOC // 2 :]], axis=0)


def unfold(a):
    rows = a.shape[0] // 2
    return jnp.concatenate([a[:rows], a[rows:]], axis=1)


LEVELS = 32767.0
BOUND = TAPS * COL * 6.0 * 0.0390625


def pack(low, high):
    low = jnp.where(low < 0, low - 0.5, low + 0.5).astype(jnp.int32)
    high = jnp.where(high < 0, high - 0.5, high + 0.5).astype(jnp.int32)
    return (high << 16) | (low & 0xFFFF)


def unpack(word):
    return ((word << 16) >> 16).astype(F32), (word >> 16).astype(F32)


def root_code(a):
    root = jnp.sqrt(jnp.sqrt(jnp.minimum(jnp.abs(a) * (1.0 / BOUND), 1.0))) * LEVELS
    return jnp.where(a < 0, -root, root)


def root_value(code):
    code = code * (1.0 / LEVELS)
    return BOUND * (code * code) * (code * jnp.abs(code))


def both(a):
    return jnp.concatenate([a, a], axis=0)


def columns_to_rows(columns):
    rows = columns[0].shape[0]
    lane = lax.broadcasted_iota(jnp.int32, (rows, 128), 1)
    out = jnp.zeros((rows, 128), F32)
    for i, column in enumerate(columns):
        out = jnp.where(lane == i, column, out)
    out = jnp.concatenate([out, jnp.zeros((128 - rows, 128), F32)], axis=0)
    return out.T[:8]


def stack_rows(rows):
    sub = lax.broadcasted_iota(jnp.int32, (8, 128), 0)
    out = jnp.zeros((8, 128), F32)
    for i, row in enumerate(rows):
        out = jnp.where(sub == i, row, out)
    return out


def rows_to_columns(rows):
    return jnp.concatenate([rows, jnp.zeros((120, 128), F32)], axis=0).T


def merge_stats(parts):
    top_d, top_t = parts[0][0:1], parts[0][3:4]
    for p in parts[1:]:
        top_d = jnp.maximum(top_d, p[0:1])
        top_t = jnp.maximum(top_t, p[3:4])
    sums = [jnp.zeros((1, 128), F32) for _ in range(5)]
    for p in parts:
        a = jnp.exp(p[0:1] - top_d)
        b = jnp.exp(p[3:4] - top_t)
        sums[0] += a * p[1:2]
        sums[1] += a * p[2:3]
        sums[2] += b * p[4:5]
        sums[3] += b * p[5:6]
        sums[4] += b * p[6:7]
    return [top_d, sums[0], sums[1], top_t, sums[2], sums[3], sums[4]]


def chain_scratch(rows):
    V, dma = pltpu.VMEM, pltpu.SemaphoreType.DMA
    i32 = jnp.int32
    padded = -(-8 * rows // 128) * 128
    half = LOC // 2
    buffers = dict(
        tapl=V((8 * rows, TAPS * COL), BF16),
        sb1=V((8, 4 * rows, COL), i32), rb1=V((8, 4 * rows, COL), i32),
        a1=V((8, rows, COL), F32), b1=V((8, rows, COL), F32), p1=V((rows, COL), F32), jy=V((8, rows, COL), F32),
        sqx=V((8, 1, padded), F32), sqb=V((8, 1, padded), F32), invc=V((8, rows, COL), F32),
        ub=V((8, 4 * rows, COL), i32), ul=V((8 * rows, LOC), BF16),
        dd=V((2, 4 * rows, LOC), F32), cr=V((4 * rows, LOC), F32), ds=V((4, rows, LOC), F32),
        zs=V((4, rows, half), i32), zr=V((4, rows, half), i32), zss=V((8, 128), F32), zsr=V((4, 8, 128), F32),
        st0=V((8, 128), F32), st1=V((8, 8, 128), F32), st2=V((8, 8, 128), F32),
        dlb=V((8, 2 * rows, half), BF16), dl=V((8 * rows, LOC), BF16), qb=V((8, 8, 128), F32),
        sb2=V((8, 8 * rows, COL), BF16), rb2=V((8, 8 * rows, COL), BF16),
        a2=V((8, rows, COL), F32), b2=V((8, rows, COL), F32), p2=V((rows, COL), F32), dn=V((8, rows, COL), F32),
        df=V((8, 8 * rows, COL), BF16),
    )
    sems = {}
    for name in ("x1", "y1", "g1", "sx", "u", "sq", "s1", "s2", "q", "x2", "y2", "g2", "df"):
        sems["s_" + name], sems["r_" + name] = dma((7,)), dma((8,))
    for name in ("z", "zs"):
        sems["s_" + name], sems["r_" + name] = dma((3,)), dma((4,))
    sems.update(s_c=dma, r_c=dma, s_dl=dma((3,)), r_dl=dma((8,)), s_fw=dma((4,)))
    return buffers | sems


def shared_scratch():
    V, dma = pltpu.VMEM, pltpu.SemaphoreType.DMA
    return dict(
        tap=V((TAPS, BLK, COL), BF16), jw=V((TAPS * COL, LOC), BF16), gain=V((8, COL), F32),
        head=V((LOC, LOC), BF16), tl=V((BLK, LOC), BF16),
        len=pltpu.SMEM((SEQS,), jnp.int32), mask=pltpu.SMEM((SEQS,), jnp.int32),
        tapg=V((8, 128, COL), BF16), ggb=V((8, 1, COL), F32),
        s_in=dma((7,)), s_tap=dma((3,)), r_tap=dma((8,)), s_tf=dma((4,)), s_gg=dma((7,)), r_gg=dma((8,)),
    )


class Names:
    def __init__(self, names, refs):
        self.__dict__.update(zip(names, refs, strict=True))


def kernel(
    tap_hbm, jw_hbm, gain_hbm, head_hbm, tl_hbm, len_hbm, mask_hbm, loss_ref, gg_ref, taps_ref, grads_ref, *scratch
):
    names = list(shared_scratch())
    m, scratch = Names(names, scratch[: len(names)]), scratch[len(names) :]
    chains = []
    for rows in SPLITS:
        names = list(chain_scratch(rows))
        chains.append(Names(names, scratch[: len(names)]))
        scratch = scratch[len(names) :]

    sec = lax.axis_index("section")
    voc = lax.axis_index("vocab")
    zh, c = lax.div(sec, 2), lax.rem(sec, 2)
    zl, y, x = lax.div(voc, 32), lax.rem(lax.div(voc, 4), 8), lax.rem(voc, 4)
    j = zl * 4 + x
    pi = c * 4 + zh

    sec_peers = []
    for a, b in ((2, 0), (2, 1), (1, 0), (3, 0), (1, 1), (3, 1), (0, 1)):
        zh2, c2 = lax.rem(zh + a, 4), lax.rem(c + b, 2)
        sec_peers.append((c2 * 4 + zh2, (zh2 * 2 + c2, voc)))
    zh_peers = []
    for a in (2, 1, 3):
        zh2 = lax.rem(zh + a, 4)
        zh_peers.append((zh2, (zh2 * 2 + c, voc)))
    near_first = zh_peers[1:] + zh_peers[:1]
    core_dev = (zh * 2 + (1 - c), voc)
    xz_peers = []
    for a, b in ((1, 2), (1, 1), (1, 3), (0, 2), (0, 1), (0, 3), (1, 0)):
        zl2, x2 = lax.rem(zl + a, 2), lax.rem(x + b, 4)
        xz_peers.append((zl2 * 4 + x2, (sec, zl2 * 32 + y * 4 + x2)))
    y_peers = []
    for a in (4, 3, 5, 2, 6, 1, 7):
        y2 = lax.rem(y + a, 8)
        y_peers.append((y2, (sec, zl * 32 + y2 * 4 + x)))

    inputs = (
        (tap_hbm, m.tap), (jw_hbm, m.jw), (gain_hbm, m.gain), (len_hbm, m.len), (mask_hbm, m.mask),
        (head_hbm, m.head), (tl_hbm, m.tl),
    )
    loads = [pltpu.make_async_copy(src, dst, m.s_in.at[i]) for i, (src, dst) in enumerate(inputs)]
    for load in loads:
        load.start()

    barrier = pltpu.get_barrier_semaphore()
    for _, dev in sec_peers + xz_peers + y_peers:
        pl.semaphore_signal(barrier, inc=1, device_id=dev, device_id_type=MESH)
    loads[0].wait()
    taps = [m.tap[k].astype(F32) for k in range(TAPS)] + [jnp.zeros((128 - TAPS * BLK, COL), F32)]
    m.tapg[pi] = jnp.concatenate(taps, axis=0).astype(BF16)
    pl.semaphore_wait(barrier, 21)

    pending = []

    def send(src, dst, s_sem, r_sem, dev):
        copy = pltpu.make_async_remote_copy(src, dst, s_sem, r_sem, device_id=dev, device_id_type=MESH)
        copy.start()
        pending.append(copy)

    def send_all(peers, src, dst, s_sem, r_sem, slot):
        for k, (other, dev) in enumerate(peers):
            send(src(other), dst.at[slot], s_sem.at[k], r_sem.at[slot], dev)

    def arrived(dst, s_sem, r_sem, dev):
        pltpu.make_async_remote_copy(dst, dst, s_sem, r_sem, device_id=dev, device_id_type=MESH).wait_recv()

    def wait_all(peers, dst, s_sem, r_sem):
        for k, (other, dev) in enumerate(peers):
            arrived(dst.at[other], s_sem.at[k], r_sem.at[other], dev)

    for k, (other, dev) in enumerate(zh_peers):
        send(m.tapg.at[pi], m.tapg.at[pi], m.s_tap.at[k], m.r_tap.at[pi], dev)
    send(m.tapg.at[pi], m.tapg.at[pi], m.s_tf.at[3], m.r_tap.at[pi], core_dev)
    for k, (other, dev) in enumerate(near_first):
        slot = c * 4 + other
        arrived(m.tapg.at[slot], m.s_tap.at[k], m.r_tap.at[slot], dev)
        send(m.tapg.at[slot], m.tapg.at[slot], m.s_tf.at[k], m.r_tap.at[slot], core_dev)
    for load in loads[1:]:
        load.wait()
    for zh2 in range(4):
        slot = (1 - c) * 4 + zh2
        arrived(m.tapg.at[slot], m.s_tf.at[0], m.r_tap.at[slot], core_dev)

    def from_roots(rb):
        low, high = [root_value(half) for half in unpack(rb[0])]
        for k in range(1, 8):
            more = [root_value(half) for half in unpack(rb[k])]
            low, high = low + more[0], high + more[1]
        return jnp.concatenate([low, high], axis=0)

    def from_bf16(rb):
        total = rb[0].astype(F32)
        for k in range(1, 8):
            total += rb[k].astype(F32)
        return total

    def vocab_sum(collect, rows, sb, rb, a_buf, b_buf, p_buf, out, s_x, r_x, s_y, r_y, s_g, r_g):
        send_all(xz_peers, lambda other: sb.at[other], rb, s_x, r_x, j)
        rb[j] = sb[j]
        yield
        wait_all(xz_peers, rb, s_x, r_x)
        total = collect(rb)
        for k in range(8):
            a_buf[k] = total[k * rows : (k + 1) * rows]
        send_all(y_peers, lambda other: a_buf.at[other], b_buf, s_y, r_y, y)
        b_buf[y] = a_buf[y]
        yield
        wait_all(y_peers, b_buf, s_y, r_y)
        piece = b_buf[0]
        for k in range(1, 8):
            piece += b_buf[k]
        p_buf[...] = piece
        send_all(y_peers, lambda other: p_buf, out, s_g, r_g, y)
        out[y] = piece
        yield
        wait_all(y_peers, out, s_g, r_g)

    results = []

    def chain(index):
        w = chains[index]
        rows, first = SPLITS[index], sum(SPLITS[:index])
        half, tokens = 4 * rows, 8 * rows
        padded = -(-tokens // 128) * 128

        blocks = [m.tapg[p].astype(F32) for p in range(8)]
        for k in range(TAPS):
            at = k * BLK + first
            tap = jnp.concatenate([b[at : at + rows] for b in blocks], axis=0)
            w.tapl[:, k * COL : (k + 1) * COL] = tap.astype(BF16)
        taps_ref[8 * first : 8 * first + tokens, :] = w.tapl[...]

        def join_step(i, carry):
            at = pl.ds(pl.multiple_of(i * 256, 256), 256)
            acc = root_code(jnp.dot(w.tapl[...], m.jw[:, at], preferred_element_type=F32))
            w.sb1[2 * i] = pack(acc[:half, :COL], acc[half:, :COL])
            w.sb1[2 * i + 1] = pack(acc[:half, COL:], acc[half:, COL:])
            return carry

        lax.fori_loop(0, 4, join_step, 0)
        yield from vocab_sum(
            from_roots, rows, w.sb1, w.rb1, w.a1, w.b1, w.p1, w.jy, w.s_x1, w.r_x1, w.s_y1, w.r_y1, w.s_g1, w.r_g1
        )

        joined = jnp.concatenate([w.jy[k] for k in range(8)], axis=0)
        square = joined * joined
        tall = square
        if padded > tokens:
            tall = jnp.concatenate([square, jnp.zeros((padded - tokens, COL), F32)], axis=0)
        w.sqx[j] = jnp.sum(tall.T, axis=0, keepdims=True)
        send_all(xz_peers, lambda other: w.sqx.at[j], w.sqx, w.s_sx, w.r_sx, j)
        code = joined * (LEVELS * lax.rsqrt(jnp.maximum(jnp.sum(square, axis=1, keepdims=True), 1e-30)))
        w.ub[j] = pack(code[:half], code[half:])
        send_all(xz_peers, lambda other: w.ub.at[j], w.ub, w.s_u, w.r_u, j)
        yield
        wait_all(xz_peers, w.sqx, w.s_sx, w.r_sx)
        square = w.sqx[0]
        for k in range(1, 8):
            square += w.sqx[k]
        w.sqb[pi] = square
        send_all(sec_peers, lambda other: w.sqb.at[pi], w.sqb, w.s_sq, w.r_sq, pi)
        yield
        wait_all(sec_peers, w.sqb, w.s_sq, w.r_sq)
        square = w.sqb[0]
        for k in range(1, 8):
            square += w.sqb[k]
        inverse = lax.rsqrt(square / WIDTH + EPS)
        factors = [jnp.sqrt(w.sqx[k]) * (1.0 / LEVELS) * inverse for k in range(8)]
        factors = jnp.concatenate(factors + [jnp.zeros((120, padded), F32)], axis=0).T
        inverse = jnp.broadcast_to(inverse, (128, padded)).T
        for k in range(8):
            w.invc[k] = inverse[k * rows : (k + 1) * rows]
        wait_all(xz_peers, w.ub, w.s_u, w.r_u)
        for k in range(8):
            for h, part in enumerate(unpack(w.ub[k])):
                normed = part * factors[h * half : (h + 1) * half, k : k + 1] * m.gain[k : k + 1, :]
                w.ul[h * half : (h + 1) * half, k * COL : (k + 1) * COL] = normed.astype(BF16)

        def draft_step(i, carry):
            at = pl.ds(pl.multiple_of(i * 256, 256), 256)
            acc = jnp.dot(w.ul[...], m.head[:, at], preferred_element_type=F32)
            w.dd[0, :, at] = acc[:half]
            w.dd[1, :, at] = acc[half:]
            return carry

        lax.fori_loop(0, 4, draft_step, 0)
        send(w.dd.at[1 - c], w.cr, w.s_c, w.r_c, core_dev)

        lane = lax.broadcasted_iota(jnp.int32, (1, 128), 1)
        valid = lane < rows
        position = sec * BLK + first + lane
        sequence = position // SPAN
        offset = position % SPAN
        length = jnp.zeros((1, 128), jnp.int32)
        keep = jnp.zeros((1, 128), jnp.int32)
        for q in range(SEQS):
            length = jnp.where(sequence == q, m.len[q], length)
            keep = jnp.where(sequence == q, m.mask[q], keep)
        live = (offset < length) & valid
        weight = jnp.where(live, keep.astype(F32) / (jnp.maximum(length, 1).astype(F32) * SEQS), 0.0)
        arrived(w.cr, w.s_c, w.r_c, core_dev)
        tops = []
        for k in range(4):
            at = slice(k * rows, (k + 1) * rows)
            part = w.dd[c, at, :] + w.cr[at, :]
            w.ds[k] = part
            tops.append(jnp.maximum(jnp.max(jnp.abs(part), axis=1, keepdims=True), 1e-30))
            code = part * (LEVELS / tops[-1])
            w.zs[k] = pack(code[:, : LOC // 2], code[:, LOC // 2 :])
        w.zss[...] = columns_to_rows(tops)
        for k, (other, dev) in enumerate(zh_peers):
            send(w.zss, w.zsr.at[zh], w.s_zs.at[k], w.r_zs.at[zh], dev)
            send(w.zs.at[other], w.zr.at[zh], w.s_z.at[k], w.r_z.at[zh], dev)
        draft = fold(w.ds[zh])
        target = fold(m.tl[...].astype(F32)[first : first + rows])
        yield
        wait_all(zh_peers, w.zsr, w.s_zs, w.r_zs)
        steps = rows_to_columns(stack_rows([w.zsr[other, pl.ds(zh, 1), :] for other, _ in zh_peers])) * (1.0 / LEVELS)
        for k, (other, dev) in enumerate(zh_peers):
            arrived(w.zr.at[other], w.s_z.at[k], w.r_z.at[other], dev)
            draft += jnp.concatenate(unpack(w.zr[other]), axis=0) * both(steps[:rows, k : k + 1])

        def per_token(a, op, reduce):
            a = op(op(a[:, :128], a[:, 128:256]), op(a[:, 256:384], a[:, 384:]))
            return reduce(op(a[:rows], a[rows:]), axis=1, keepdims=True)

        def top(a):
            return per_token(a, jnp.maximum, jnp.max)

        def add(a):
            return per_token(a, jnp.add, jnp.sum)

        d_top = top(draft)
        d_exp = jnp.exp(draft - both(d_top))
        t_top = top(target)
        t_exp = jnp.exp(target - both(t_top))
        w.st0[...] = columns_to_rows(
            [d_top, add(d_exp), add(d_exp * draft), t_top, add(t_exp), add(t_exp * (target - draft)), add(t_exp * draft)]
        )
        send_all(xz_peers, lambda other: w.st0, w.st1, w.s_s1, w.r_s1, j)
        w.st1[j] = w.st0[...]
        yield
        wait_all(xz_peers, w.st1, w.s_s1, w.r_s1)
        w.st2[y] = stack_rows(merge_stats([w.st1[k] for k in range(8)]))
        send_all(y_peers, lambda other: w.st2.at[y], w.st2, w.s_s2, w.r_s2, y)
        yield
        wait_all(y_peers, w.st2, w.s_s2, w.r_s2)
        d_top, d_sum, d_first, t_top, t_sum, cross, t_first = merge_stats([w.st2[k] for k in range(8)])
        d_sum = jnp.where(valid, d_sum, 1.0)
        t_sum = jnp.where(valid, t_sum, 1.0)
        d_lse = d_top + jnp.log(d_sum)
        t_lse = t_top + jnp.log(t_sum)
        loss = weight * (cross / t_sum - t_lse + d_lse)
        scale = LOSS_SCALE * weight
        along = scale * (d_first / d_sum - t_first / t_sum)
        cols = rows_to_columns(stack_rows([d_lse, scale, t_top, scale / t_sum]))[:rows]
        dlogit = both(cols[:, 1:2]) * jnp.exp(draft - both(cols[:, 0:1]))
        dlogit -= both(cols[:, 3:4]) * jnp.exp(target - both(cols[:, 2:3]))
        w.dlb[pi] = dlogit.astype(BF16)
        for k, (other, dev) in enumerate(zh_peers):
            send(w.dlb.at[pi], w.dlb.at[pi], w.s_dl.at[k], w.r_dl.at[pi], dev)
        send(w.dlb.at[pi], w.dlb.at[pi], w.s_fw.at[3], w.r_dl.at[pi], core_dev)
        w.qb[pi] = stack_rows([along, loss])
        send_all(sec_peers, lambda other: w.qb.at[pi], w.qb, w.s_q, w.r_q, pi)
        yield
        for k, (other, dev) in enumerate(near_first):
            slot = c * 4 + other
            arrived(w.dlb.at[slot], w.s_dl.at[k], w.r_dl.at[slot], dev)
            send(w.dlb.at[slot], w.dlb.at[slot], w.s_fw.at[k], w.r_dl.at[slot], core_dev)
        for zh2 in range(4):
            slot = (1 - c) * 4 + zh2
            arrived(w.dlb.at[slot], w.s_fw.at[0], w.r_dl.at[slot], core_dev)
        for k in range(0, 8, 2):
            pair = [unfold(w.dlb[k + i].astype(F32)) for i in range(2)]
            w.dl[k * rows : (k + 2) * rows] = jnp.concatenate(pair, axis=0).astype(BF16)

        def grad_step(i, carry):
            at = pl.ds(pl.multiple_of(i * 256, 256), 256)
            acc = lax.dot_general(w.dl[...], m.head[at, :], (((1,), (1,)), ((), ())), preferred_element_type=F32)
            w.sb2[2 * i] = acc[:, :COL].astype(BF16)
            w.sb2[2 * i + 1] = acc[:, COL:].astype(BF16)
            return carry

        lax.fori_loop(0, 4, grad_step, 0)
        yield from vocab_sum(
            from_bf16, rows, w.sb2, w.rb2, w.a2, w.b2, w.p2, w.dn, w.s_x2, w.r_x2, w.s_y2, w.r_y2, w.s_g2, w.r_g2
        )

        wait_all(sec_peers, w.qb, w.s_q, w.r_q)
        loss = w.qb[0, 1:2]
        for k in range(1, 8):
            loss += w.qb[k, 1:2]
        q_cols = rows_to_columns(stack_rows([w.qb[k, 0:1] for k in range(8)]))[:rows]
        gain = m.gain[pl.ds(j, 1), :]
        gg = jnp.zeros((rows, COL), F32)
        pair = []
        for k in range(8):
            inv = w.invc[k]
            joined = w.jy[k]
            grad = w.dn[k] * inv
            gg += grad * joined
            pair.append(grad * gain - joined * (q_cols[:, k : k + 1] * inv * inv / WIDTH))
            if k % 2:
                w.df[j, (k - 1) * rows : (k + 1) * rows] = jnp.concatenate(pair, axis=0).astype(BF16)
                pair = []
        send_all(xz_peers, lambda other: w.df.at[j], w.df, w.s_df, w.r_df, j)
        results.append((loss, jnp.sum(gg, axis=0, keepdims=True)))
        if index == len(SPLITS) - 1:
            m.ggb[j] = sum(gg for _, gg in results)
            send_all(xz_peers, lambda other: m.ggb.at[j], m.ggb, m.s_gg, m.r_gg, j)
            loss_ref[0, 0] = jnp.sum(sum(loss for loss, _ in results))
        yield
        wait_all(xz_peers, w.df, w.s_df, w.r_df)
        for k in range(8):
            grads_ref[8 * first : 8 * first + tokens, k * COL : (k + 1) * COL] = w.df[k]

    running = [chain(i) for i in range(len(SPLITS))]
    while running:
        running = [one for one in running if next(one, running) is not running]
    wait_all(xz_peers, m.ggb, m.s_gg, m.r_gg)
    for k in range(8):
        gg_ref[k : k + 1, :] = m.ggb[k]
    for copy in pending:
        copy.wait_send()


def last_kernel(taps_ref, grads_ref, gg_in, loss_in, out_ref, gg_ref, loss_ref):
    out_ref[...] = lax.dot_general(
        taps_ref[...], grads_ref[...], (((0,), (0,)), ((), ())), preferred_element_type=F32
    )
    gg_ref[...] = gg_in[...]
    loss_ref[0, 0] = loss_in[0, 0]


def shards(tap_hidden, join_weight, norm_gain, head_weight, target_logits, seq_lengths, seq_mask):
    vmem = pl.BlockSpec(memory_space=pltpu.VMEM)
    smem = pl.BlockSpec(memory_space=pltpu.SMEM)
    hbm = pl.BlockSpec(memory_space=pl.ANY)
    scratch = list(shared_scratch().values())
    for rows in SPLITS:
        scratch += list(chain_scratch(rows).values())
    loss, gain_grad, taps, grads = pl.pallas_call(
        kernel,
        out_shape=(
            jax.ShapeDtypeStruct((1, 1), F32),
            jax.ShapeDtypeStruct((8, COL), F32),
            jax.ShapeDtypeStruct((TOK, TAPS * COL), BF16),
            jax.ShapeDtypeStruct((TOK, LOC), BF16),
        ),
        in_specs=[hbm] * 7,
        out_specs=(smem, vmem, vmem, vmem),
        scratch_shapes=scratch,
        compiler_params=pltpu.CompilerParams(
            collective_id=0, has_side_effects=True, vmem_limit_bytes=60 * 1024 * 1024
        ),
        name="draft_step",
    )(
        tap_hidden,
        join_weight.reshape(TAPS * COL, LOC),
        norm_gain.reshape(8, COL),
        head_weight,
        target_logits,
        seq_lengths,
        seq_mask,
    )
    tile = 256
    join_grad, gain_grad, loss = pl.pallas_call(
        last_kernel,
        grid=(LOC // tile,),
        out_shape=(
            jax.ShapeDtypeStruct((TAPS * COL, LOC), F32),
            jax.ShapeDtypeStruct((8, COL), F32),
            jax.ShapeDtypeStruct((1, 1), F32),
        ),
        in_specs=[
            pl.BlockSpec((TOK, TAPS * COL), lambda i: (0, 0)),
            pl.BlockSpec((TOK, tile), lambda i: (0, i)),
            pl.BlockSpec((8, COL), lambda i: (0, 0)),
            smem,
        ],
        out_specs=(
            pl.BlockSpec((TAPS * COL, tile), lambda i: (0, i)),
            pl.BlockSpec((8, COL), lambda i: (0, 0)),
            smem,
        ),
        compiler_params=pltpu.CompilerParams(vmem_limit_bytes=60 * 1024 * 1024),
        name="join_gradient",
    )(taps, grads, gain_grad, loss)
    return loss.reshape(()), join_grad.reshape(TAPS, COL, LOC), gain_grad.reshape(LOC)


def solution(mesh):
    in_specs = (
        P(None, "section", "vocab"),
        P(None, "vocab", "section"),
        P("section"),
        P("section", "vocab"),
        P("section", "vocab"),
        P(),
        P(),
    )
    out_specs = (P(), P(None, "vocab", "section"), P("section"))
    return jax.shard_map(shards, mesh=mesh, in_specs=in_specs, out_specs=out_specs, check_vma=False)
```

time: 133 us -> 116 us (0.87)
  Pallas kernels: 127 us -> 115 us
  local copies, waits for them, and re-layouts: 3.33 us -> 0 us
  between operations: 2.41 us -> 0.64 us
    pallas_call x1, Pallas kernels: 127 us -> 110 us  [shards(): pl.pallas_call(kernel, out_shape=(jax.ShapeDtypeStruct((1, 1), F32), jax....]
    pallas_call x0 -> x1, Pallas kernels: none -> 4.7 us  [shards(): pl.pallas_call(last_kernel, grid=(LOC // tile,), out_shape=(jax.ShapeDtyp...]
    unnamed x4 -> x0, local copies, waits for them, and re-layouts: 3.33 us -> none
where the time goes in v3:
time: 116 us
  Pallas kernels  115 us (99%)
    pallas_call x1, Pallas kernels, shards(): pl.pallas_call(kernel, out_shape=(jax.ShapeDtypeStruct((1, 1), F32), jax....  110 us
    pallas_call x1, Pallas kernels, shards(): pl.pallas_call(last_kernel, grid=(LOC // tile,), out_shape=(jax.ShapeDtyp...  4.7 us

profile of v3, /device:TPU:1, one launch (start us, length us, event | category | flops | bytes accessed | tf_op | source)
XLA Modules:
  0.0 115.7 jit_solution(3064183333545253225)
XLA Ops:
  0.6 110.4 %draft_step.1 = (f32[1,1]{1,0:T(1,128)}, f32[8,128]{1,0:T(8,128)}, bf16[320,384]{1,0:T(8,128)(2,1)}, bf16[320,1024]{1,0:T(8,128)(2,1)}) custom-call(bf16[3,40,128]{2,1,0:T(8,128)(2,1)} %tap_hbm.1, bf16[384,1024]{1,0:T(8,128)(2,1)} %bitcast.5, f32[8,128]{1,0:T(8,128)} %bitcast.6, bf16[1024,1024]{1,0:T(8,128)(2,1)} %head_hbm.1, bf16[40,1024]{1,0:T(8,128)(2,1)} %tl_hbm.1, ...), custom_call_target="tpu_custom_call" | custom-call | tf_op jit(solution)/shard_map/draft_step/pallas_call | solution.py:487
  111.0 4.7 %join_gradient.1 = (f32[384,1024]{1,0:T(8,128)}, f32[8,128]{1,0:T(8,128)}, f32[1,1]{1,0:T(1,128)}) custom-call(bf16[320,384]{1,0:T(8,128)(2,1)} %get-tuple-element.10.taps_ref, bf16[320,1024]{1,0:T(8,128)(2,1)} %get-tuple-element.11.grads_ref, f32[8,128]{1,0:T(8,128)} %get-tuple-element.12.gg_in, f32[1,1]{1,0:T(1,128)} %get-tuple-element.13.loss_in), custom_call_target="tpu_custom_call" | custom-call | tf_op jit(solution)/shard_map/join_gradient/pallas_call | solution.py:512

commit v4 on v3

--- a/solution.py
+++ b/solution.py
@@ -117,12 +117,9 @@
         a2=V((8, rows, COL), F32), b2=V((8, rows, COL), F32), p2=V((rows, COL), F32), dn=V((8, rows, COL), F32),
         df=V((8, 8 * rows, COL), BF16),
     )
-    sems = {}
-    for name in ("x1", "y1", "g1", "sx", "u", "sq", "s1", "s2", "q", "x2", "y2", "g2", "df"):
-        sems["s_" + name], sems["r_" + name] = dma((7,)), dma((8,))
-    for name in ("z", "zs"):
-        sems["s_" + name], sems["r_" + name] = dma((3,)), dma((4,))
-    sems.update(s_c=dma, r_c=dma, s_dl=dma((3,)), r_dl=dma((8,)), s_fw=dma((4,)))
+    names = ("x1", "y1", "g1", "sx", "u", "sq", "s1", "s2", "q", "x2", "y2", "g2", "df", "z", "zs", "c", "fw")
+    sems = {side + name: dma for name in names for side in ("s_", "r_")}
+    sems.update(s_dl=dma, r_dl=dma((4,)))
     return buffers | sems
 
 
@@ -133,7 +130,7 @@
         head=V((LOC, LOC), BF16), tl=V((BLK, LOC), BF16),
         len=pltpu.SMEM((SEQS,), jnp.int32), mask=pltpu.SMEM((SEQS,), jnp.int32),
         tapg=V((8, 128, COL), BF16), ggb=V((8, 1, COL), F32),
-        s_in=dma((7,)), s_tap=dma((3,)), r_tap=dma((8,)), s_tf=dma((4,)), s_gg=dma((7,)), r_gg=dma((8,)),
+        s_in=dma((7,)), s_tap=dma, r_tap=dma((4,)), s_tf=dma, r_tf=dma, s_gg=dma, r_gg=dma,
     )
 
 
@@ -195,36 +192,46 @@
     m.tapg[pi] = jnp.concatenate(taps, axis=0).astype(BF16)
     pl.semaphore_wait(barrier, 21)
 
-    pending = []
-
-    def send(src, dst, s_sem, r_sem, dev):
-        copy = pltpu.make_async_remote_copy(src, dst, s_sem, r_sem, device_id=dev, device_id_type=MESH)
-        copy.start()
-        pending.append(copy)
+    def copy_to(src, dst, s_sem, r_sem, dev):
+        return pltpu.make_async_remote_copy(src, dst, s_sem, r_sem, device_id=dev, device_id_type=MESH)
+
+    sent = []
 
     def send_all(peers, src, dst, s_sem, r_sem, slot):
-        for k, (other, dev) in enumerate(peers):
-            send(src(other), dst.at[slot], s_sem.at[k], r_sem.at[slot], dev)
-
-    def arrived(dst, s_sem, r_sem, dev):
-        pltpu.make_async_remote_copy(dst, dst, s_sem, r_sem, device_id=dev, device_id_type=MESH).wait_recv()
+        for other, dev in peers:
+            copy_to(src(other), dst.at[slot], s_sem, r_sem, dev).start()
+        whole = dst.at[pl.ds(0, len(peers))]
+        sent.append(copy_to(whole, whole, s_sem, r_sem, peers[0][1]))
+
+    def settle(first):
+        for copy in sent[:first]:
+            copy.wait_send()
+        del sent[:first]
 
     def wait_all(peers, dst, s_sem, r_sem):
-        for k, (other, dev) in enumerate(peers):
-            arrived(dst.at[other], s_sem.at[k], r_sem.at[other], dev)
-
-    for k, (other, dev) in enumerate(zh_peers):
-        send(m.tapg.at[pi], m.tapg.at[pi], m.s_tap.at[k], m.r_tap.at[pi], dev)
-    send(m.tapg.at[pi], m.tapg.at[pi], m.s_tf.at[3], m.r_tap.at[pi], core_dev)
-    for k, (other, dev) in enumerate(near_first):
-        slot = c * 4 + other
-        arrived(m.tapg.at[slot], m.s_tap.at[k], m.r_tap.at[slot], dev)
-        send(m.tapg.at[slot], m.tapg.at[slot], m.s_tf.at[k], m.r_tap.at[slot], core_dev)
+        whole = dst.at[pl.ds(0, len(peers))]
+        copy_to(whole, whole, s_sem, r_sem, peers[0][1]).wait_recv()
+
+    def spread(buf, s_near, r_near, s_core, r_core):
+        for other, dev in zh_peers:
+            copy_to(buf.at[pi], buf.at[pi], s_near, r_near.at[zh], dev).start()
+        copy_to(buf.at[pi], buf.at[pi], s_core, r_core, core_dev).start()
+
+    def relay(buf, s_near, r_near, s_core, r_core):
+        for other, dev in near_first:
+            slot = c * 4 + other
+            copy_to(buf.at[slot], buf.at[slot], s_near, r_near.at[other], dev).wait_recv()
+            copy_to(buf.at[slot], buf.at[slot], s_core, r_core, core_dev).start()
+        three, four = buf.at[pl.ds(0, 3)], buf.at[pl.ds(0, 4)]
+        copy_to(three, three, s_near, r_near.at[0], core_dev).wait_send()
+        last = copy_to(four, four, s_core, r_core, core_dev)
+        last.wait_recv()
+        sent.append(last)
+
+    spread(m.tapg, m.s_tap, m.r_tap, m.s_tf, m.r_tf)
     for load in loads[1:]:
         load.wait()
-    for zh2 in range(4):
-        slot = (1 - c) * 4 + zh2
-        arrived(m.tapg.at[slot], m.s_tf.at[0], m.r_tap.at[slot], core_dev)
+    relay(m.tapg, m.s_tap, m.r_tap, m.s_tf, m.r_tf)
 
     def from_roots(rb):
         low, high = [root_value(half) for half in unpack(rb[0])]
@@ -329,7 +336,8 @@
             return carry
 
         lax.fori_loop(0, 4, draft_step, 0)
-        send(w.dd.at[1 - c], w.cr, w.s_c, w.r_c, core_dev)
+        across = copy_to(w.dd.at[1 - c], w.cr, w.s_c, w.r_c, core_dev)
+        across.start()
 
         lane = lax.broadcasted_iota(jnp.int32, (1, 128), 1)
         valid = lane < rows
@@ -343,7 +351,7 @@
             keep = jnp.where(sequence == q, m.mask[q], keep)
         live = (offset < length) & valid
         weight = jnp.where(live, keep.astype(F32) / (jnp.maximum(length, 1).astype(F32) * SEQS), 0.0)
-        arrived(w.cr, w.s_c, w.r_c, core_dev)
+        across.wait_recv()
         tops = []
         for k in range(4):
             at = slice(k * rows, (k + 1) * rows)
@@ -353,16 +361,16 @@
             code = part * (LEVELS / tops[-1])
             w.zs[k] = pack(code[:, : LOC // 2], code[:, LOC // 2 :])
         w.zss[...] = columns_to_rows(tops)
-        for k, (other, dev) in enumerate(zh_peers):
-            send(w.zss, w.zsr.at[zh], w.s_zs.at[k], w.r_zs.at[zh], dev)
-            send(w.zs.at[other], w.zr.at[zh], w.s_z.at[k], w.r_z.at[zh], dev)
+        send_all(zh_peers, lambda other: w.zss, w.zsr, w.s_zs, w.r_zs, zh)
+        send_all(zh_peers, lambda other: w.zs.at[other], w.zr, w.s_z, w.r_z, zh)
+        across.wait_send()
         draft = fold(w.ds[zh])
         target = fold(m.tl[...].astype(F32)[first : first + rows])
         yield
         wait_all(zh_peers, w.zsr, w.s_zs, w.r_zs)
         steps = rows_to_columns(stack_rows([w.zsr[other, pl.ds(zh, 1), :] for other, _ in zh_peers])) * (1.0 / LEVELS)
-        for k, (other, dev) in enumerate(zh_peers):
-            arrived(w.zr.at[other], w.s_z.at[k], w.r_z.at[other], dev)
+        wait_all(zh_peers, w.zr, w.s_z, w.r_z)
+        for k, (other, _) in enumerate(zh_peers):
             draft += jnp.concatenate(unpack(w.zr[other]), axis=0) * both(steps[:rows, k : k + 1])
 
         def per_token(a, op, reduce):
@@ -402,19 +410,11 @@
         dlogit = both(cols[:, 1:2]) * jnp.exp(draft - both(cols[:, 0:1]))
         dlogit -= both(cols[:, 3:4]) * jnp.exp(target - both(cols[:, 2:3]))
         w.dlb[pi] = dlogit.astype(BF16)
-        for k, (other, dev) in enumerate(zh_peers):
-            send(w.dlb.at[pi], w.dlb.at[pi], w.s_dl.at[k], w.r_dl.at[pi], dev)
-        send(w.dlb.at[pi], w.dlb.at[pi], w.s_fw.at[3], w.r_dl.at[pi], core_dev)
+        spread(w.dlb, w.s_dl, w.r_dl, w.s_fw, w.r_fw)
         w.qb[pi] = stack_rows([along, loss])
         send_all(sec_peers, lambda other: w.qb.at[pi], w.qb, w.s_q, w.r_q, pi)
         yield
-        for k, (other, dev) in enumerate(near_first):
-            slot = c * 4 + other
-            arrived(w.dlb.at[slot], w.s_dl.at[k], w.r_dl.at[slot], dev)
-            send(w.dlb.at[slot], w.dlb.at[slot], w.s_fw.at[k], w.r_dl.at[slot], core_dev)
-        for zh2 in range(4):
-            slot = (1 - c) * 4 + zh2
-            arrived(w.dlb.at[slot], w.s_fw.at[0], w.r_dl.at[slot], core_dev)
+        relay(w.dlb, w.s_dl, w.r_dl, w.s_fw, w.r_fw)
         for k in range(0, 8, 2):
             pair = [unfold(w.dlb[k + i].astype(F32)) for i in range(2)]
             w.dl[k * rows : (k + 2) * rows] = jnp.concatenate(pair, axis=0).astype(BF16)
@@ -461,12 +461,13 @@
 
     running = [chain(i) for i in range(len(SPLITS))]
     while running:
+        before = len(sent)
         running = [one for one in running if next(one, running) is not running]
+        settle(before)
     wait_all(xz_peers, m.ggb, m.s_gg, m.r_gg)
     for k in range(8):
         gg_ref[k : k + 1, :] = m.ggb[k]
-    for copy in pending:
-        copy.wait_send()
+    settle(len(sent))
 
 
 def last_kernel(taps_ref, grads_ref, gg_in, loss_in, out_ref, gg_ref, loss_ref):

time: 116 us -> 110 us (0.948)
  Pallas kernels: 115 us -> 109 us
    pallas_call x1, Pallas kernels: 110 us -> 105 us  [shards(): pl.pallas_call(kernel, out_shape=(jax.ShapeDtypeStruct((1, 1), F32), jax....]
where the time goes in v4:
time: 110 us
  Pallas kernels  109 us (99%)
    pallas_call x1, Pallas kernels, shards(): pl.pallas_call(kernel, out_shape=(jax.ShapeDtypeStruct((1, 1), F32), jax....  105 us
    pallas_call x1, Pallas kernels, shards(): pl.pallas_call(last_kernel, grid=(LOC // tile,), out_shape=(jax.ShapeDtyp...  4.7 us

profile of v4, /device:TPU:1, one launch (start us, length us, event | category | flops | bytes accessed | tf_op | source)
XLA Modules:
  0.0 110.0 jit_solution(6811394747508189916)
XLA Ops:
  0.6 104.6 %draft_step.1 = (f32[1,1]{1,0:T(1,128)}, f32[8,128]{1,0:T(8,128)}, bf16[320,384]{1,0:T(8,128)(2,1)}, bf16[320,1024]{1,0:T(8,128)(2,1)}) custom-call(bf16[3,40,128]{2,1,0:T(8,128)(2,1)} %tap_hbm.1, bf16[384,1024]{1,0:T(8,128)(2,1)} %bitcast.5, f32[8,128]{1,0:T(8,128)} %bitcast.6, bf16[1024,1024]{1,0:T(8,128)(2,1)} %head_hbm.1, bf16[40,1024]{1,0:T(8,128)(2,1)} %tl_hbm.1, ...), custom_call_target="tpu_custom_call" | custom-call | tf_op jit(solution)/shard_map/draft_step/pallas_call | solution.py:488
  105.2 4.7 %join_gradient.1 = (f32[384,1024]{1,0:T(8,128)}, f32[8,128]{1,0:T(8,128)}, f32[1,1]{1,0:T(1,128)}) custom-call(bf16[320,384]{1,0:T(8,128)(2,1)} %get-tuple-element.10.taps_ref, bf16[320,1024]{1,0:T(8,128)(2,1)} %get-tuple-element.11.grads_ref, f32[8,128]{1,0:T(8,128)} %get-tuple-element.12.gg_in, f32[1,1]{1,0:T(1,128)} %get-tuple-element.13.loss_in), custom_call_target="tpu_custom_call" | custom-call | tf_op jit(solution)/shard_map/join_gradient/pallas_call | solution.py:513

commit v5 on v4

--- a/solution.py
+++ b/solution.py
@@ -98,26 +98,30 @@
     return [top_d, sums[0], sums[1], top_t, sums[2], sums[3], sums[4]]
 
 
+def pad128(tokens):
+    return -(-tokens // 128) * 128
+
+
 def chain_scratch(rows):
     V, dma = pltpu.VMEM, pltpu.SemaphoreType.DMA
     i32 = jnp.int32
-    padded = -(-8 * rows // 128) * 128
+    padded = pad128(8 * rows)
     half = LOC // 2
     buffers = dict(
-        tapl=V((8 * rows, TAPS * COL), BF16),
+        tapl=V((8 * rows, TAPS * COL), BF16), tapt=V((TAPS * COL, padded), BF16), dfl=V((padded, LOC), BF16),
         sb1=V((8, 4 * rows, COL), i32), rb1=V((8, 4 * rows, COL), i32),
         a1=V((8, rows, COL), F32), b1=V((8, rows, COL), F32), p1=V((rows, COL), F32), jy=V((8, rows, COL), F32),
         sqx=V((8, 1, padded), F32), sqb=V((8, 1, padded), F32), invc=V((8, rows, COL), F32),
         ub=V((8, 4 * rows, COL), i32), ul=V((8 * rows, LOC), BF16),
-        dd=V((2, 4 * rows, LOC), F32), cr=V((4 * rows, LOC), F32), ds=V((4, rows, LOC), F32),
+        dd=V((2, 4, 4 * rows, 256), F32), cr=V((4, 4 * rows, 256), F32), ds=V((4, rows, LOC), F32),
         zs=V((4, rows, half), i32), zr=V((4, rows, half), i32), zss=V((8, 128), F32), zsr=V((4, 8, 128), F32),
         st0=V((8, 128), F32), st1=V((8, 8, 128), F32), st2=V((8, 8, 128), F32),
-        dlb=V((8, 2 * rows, half), BF16), dl=V((8 * rows, LOC), BF16), qb=V((8, 8, 128), F32),
+        dlb=V((8, 2 * rows, half), BF16), dl=V((8 * rows, LOC), BF16),
         sb2=V((8, 8 * rows, COL), BF16), rb2=V((8, 8 * rows, COL), BF16),
         a2=V((8, rows, COL), F32), b2=V((8, rows, COL), F32), p2=V((rows, COL), F32), dn=V((8, rows, COL), F32),
         df=V((8, 8 * rows, COL), BF16),
     )
-    names = ("x1", "y1", "g1", "sx", "u", "sq", "s1", "s2", "q", "x2", "y2", "g2", "df", "z", "zs", "c", "fw")
+    names = ("x1", "y1", "g1", "sx", "u", "sq", "s1", "s2", "x2", "y2", "g2", "df", "z", "zs", "c", "fw")
     sems = {side + name: dma for name in names for side in ("s_", "r_")}
     sems.update(s_dl=dma, r_dl=dma((4,)))
     return buffers | sems
@@ -129,8 +133,8 @@
         tap=V((TAPS, BLK, COL), BF16), jw=V((TAPS * COL, LOC), BF16), gain=V((8, COL), F32),
         head=V((LOC, LOC), BF16), tl=V((BLK, LOC), BF16),
         len=pltpu.SMEM((SEQS,), jnp.int32), mask=pltpu.SMEM((SEQS,), jnp.int32),
-        tapg=V((8, 128, COL), BF16), ggb=V((8, 1, COL), F32),
-        s_in=dma((7,)), s_tap=dma, r_tap=dma((4,)), s_tf=dma, r_tf=dma, s_gg=dma, r_gg=dma,
+        tapg=V((8, 128, COL), BF16), ggb=V((8, 1, COL), F32), qb=V((8, 1, 128), F32),
+        s_in=dma((7,)), s_tap=dma, r_tap=dma((4,)), s_tf=dma, r_tf=dma, s_gg=dma, r_gg=dma, s_q=dma, r_q=dma,
     )
 
 
@@ -140,7 +144,7 @@
 
 
 def kernel(
-    tap_hbm, jw_hbm, gain_hbm, head_hbm, tl_hbm, len_hbm, mask_hbm, loss_ref, gg_ref, taps_ref, grads_ref, *scratch
+    tap_hbm, jw_hbm, gain_hbm, head_hbm, tl_hbm, len_hbm, mask_hbm, loss_ref, gg_ref, out_ref, *scratch
 ):
     names = list(shared_scratch())
     m, scratch = Names(names, scratch[: len(names)]), scratch[len(names) :]
@@ -246,9 +250,11 @@
             total += rb[k].astype(F32)
         return total
 
-    def vocab_sum(collect, rows, sb, rb, a_buf, b_buf, p_buf, out, s_x, r_x, s_y, r_y, s_g, r_g):
+    def vocab_sum(collect, rows, sb, rb, a_buf, b_buf, p_buf, out, s_x, r_x, s_y, r_y, s_g, r_g, between=None):
         send_all(xz_peers, lambda other: sb.at[other], rb, s_x, r_x, j)
         rb[j] = sb[j]
+        if between is not None:
+            between()
         yield
         wait_all(xz_peers, rb, s_x, r_x)
         total = collect(rb)
@@ -267,20 +273,20 @@
         yield
         wait_all(y_peers, out, s_g, r_g)
 
-    results = []
+    gain_rows = []
+    per_token_rows = []
 
     def chain(index):
         w = chains[index]
         rows, first = SPLITS[index], sum(SPLITS[:index])
         half, tokens = 4 * rows, 8 * rows
-        padded = -(-tokens // 128) * 128
+        padded = pad128(tokens)
 
         blocks = [m.tapg[p].astype(F32) for p in range(8)]
         for k in range(TAPS):
             at = k * BLK + first
             tap = jnp.concatenate([b[at : at + rows] for b in blocks], axis=0)
             w.tapl[:, k * COL : (k + 1) * COL] = tap.astype(BF16)
-        taps_ref[8 * first : 8 * first + tokens, :] = w.tapl[...]
 
         def join_step(i, carry):
             at = pl.ds(pl.multiple_of(i * 256, 256), 256)
@@ -290,8 +296,19 @@
             return carry
 
         lax.fori_loop(0, 4, join_step, 0)
+
+        def turn_taps():
+            for k in range(TAPS):
+                tap = w.tapl[:, k * COL : (k + 1) * COL].astype(F32)
+                if padded > tokens:
+                    tap = jnp.concatenate([tap, jnp.zeros((padded - tokens, COL), F32)], axis=0)
+                w.tapt[k * COL : (k + 1) * COL, :] = tap.T.astype(BF16)
+            if padded > tokens:
+                w.dfl[tokens:, :] = jnp.zeros((padded - tokens, LOC), BF16)
+
         yield from vocab_sum(
-            from_roots, rows, w.sb1, w.rb1, w.a1, w.b1, w.p1, w.jy, w.s_x1, w.r_x1, w.s_y1, w.r_y1, w.s_g1, w.r_g1
+            from_roots, rows, w.sb1, w.rb1, w.a1, w.b1, w.p1, w.jy, w.s_x1, w.r_x1, w.s_y1, w.r_y1, w.s_g1, w.r_g1,
+            between=turn_taps,
         )
 
         joined = jnp.concatenate([w.jy[k] for k in range(8)], axis=0)
@@ -331,13 +348,13 @@
         def draft_step(i, carry):
             at = pl.ds(pl.multiple_of(i * 256, 256), 256)
             acc = jnp.dot(w.ul[...], m.head[:, at], preferred_element_type=F32)
-            w.dd[0, :, at] = acc[:half]
-            w.dd[1, :, at] = acc[half:]
+            w.dd[0, i] = acc[:half]
+            w.dd[1, i] = acc[half:]
+            copy_to(w.dd.at[1 - c, i], w.cr.at[i], w.s_c, w.r_c, core_dev).start()
             return carry
 
         lax.fori_loop(0, 4, draft_step, 0)
-        across = copy_to(w.dd.at[1 - c], w.cr, w.s_c, w.r_c, core_dev)
-        across.start()
+        across = copy_to(w.cr, w.cr, w.s_c, w.r_c, core_dev)
 
         lane = lax.broadcasted_iota(jnp.int32, (1, 128), 1)
         valid = lane < rows
@@ -355,7 +372,7 @@
         tops = []
         for k in range(4):
             at = slice(k * rows, (k + 1) * rows)
-            part = w.dd[c, at, :] + w.cr[at, :]
+            part = jnp.concatenate([w.dd[c, i, at, :] + w.cr[i, at, :] for i in range(4)], axis=1)
             w.ds[k] = part
             tops.append(jnp.maximum(jnp.max(jnp.abs(part), axis=1, keepdims=True), 1e-30))
             code = part * (LEVELS / tops[-1])
@@ -411,8 +428,12 @@
         dlogit -= both(cols[:, 3:4]) * jnp.exp(target - both(cols[:, 2:3]))
         w.dlb[pi] = dlogit.astype(BF16)
         spread(w.dlb, w.s_dl, w.r_dl, w.s_fw, w.r_fw)
-        w.qb[pi] = stack_rows([along, loss])
-        send_all(sec_peers, lambda other: w.qb.at[pi], w.qb, w.s_q, w.r_q, pi)
+        for row, at in ((along, first), (loss, first + 64)):
+            row = jnp.broadcast_to(row, (8, 128))
+            per_token_rows.append((pltpu.roll(row, at, 1) if at else row)[0:1])
+        if index == len(SPLITS) - 1:
+            m.qb[pi] = sum(per_token_rows)
+            send_all(sec_peers, lambda other: m.qb.at[pi], m.qb, m.s_q, m.r_q, pi)
         yield
         relay(w.dlb, w.s_dl, w.r_dl, w.s_fw, w.r_fw)
         for k in range(0, 8, 2):
@@ -431,11 +452,13 @@
             from_bf16, rows, w.sb2, w.rb2, w.a2, w.b2, w.p2, w.dn, w.s_x2, w.r_x2, w.s_y2, w.r_y2, w.s_g2, w.r_g2
         )
 
-        wait_all(sec_peers, w.qb, w.s_q, w.r_q)
-        loss = w.qb[0, 1:2]
-        for k in range(1, 8):
-            loss += w.qb[k, 1:2]
-        q_cols = rows_to_columns(stack_rows([w.qb[k, 0:1] for k in range(8)]))[:rows]
+        if index == 0:
+            wait_all(sec_peers, m.qb, m.s_q, m.r_q)
+            gathered = m.qb[0]
+            for k in range(1, 8):
+                gathered += m.qb[k]
+            loss_ref[0, 0] = jnp.sum(jnp.where(lax.broadcasted_iota(jnp.int32, (1, 128), 1) < 64, 0.0, gathered))
+        q_cols = rows_to_columns(stack_rows([m.qb[k] for k in range(8)]))[first : first + rows]
         gain = m.gain[pl.ds(j, 1), :]
         gg = jnp.zeros((rows, COL), F32)
         pair = []
@@ -449,15 +472,22 @@
                 w.df[j, (k - 1) * rows : (k + 1) * rows] = jnp.concatenate(pair, axis=0).astype(BF16)
                 pair = []
         send_all(xz_peers, lambda other: w.df.at[j], w.df, w.s_df, w.r_df, j)
-        results.append((loss, jnp.sum(gg, axis=0, keepdims=True)))
+        gain_rows.append(jnp.sum(gg, axis=0, keepdims=True))
         if index == len(SPLITS) - 1:
-            m.ggb[j] = sum(gg for _, gg in results)
+            m.ggb[j] = sum(gain_rows)
             send_all(xz_peers, lambda other: m.ggb.at[j], m.ggb, m.s_gg, m.r_gg, j)
-            loss_ref[0, 0] = jnp.sum(sum(loss for loss, _ in results))
         yield
         wait_all(xz_peers, w.df, w.s_df, w.r_df)
         for k in range(8):
-            grads_ref[8 * first : 8 * first + tokens, k * COL : (k + 1) * COL] = w.df[k]
+            w.dfl[:tokens, k * COL : (k + 1) * COL] = w.df[k]
+
+        def out_step(i, carry):
+            at = pl.ds(pl.multiple_of(i * 256, 256), 256)
+            part = jnp.dot(w.tapt[...], w.dfl[:, at], preferred_element_type=F32)
+            out_ref[:, at] = part if index == 0 else out_ref[:, at] + part
+            return carry
+
+        lax.fori_loop(0, 4, out_step, 0)
 
     running = [chain(i) for i in range(len(SPLITS))]
     while running:
@@ -470,14 +500,6 @@
     settle(len(sent))
 
 
-def last_kernel(taps_ref, grads_ref, gg_in, loss_in, out_ref, gg_ref, loss_ref):
-    out_ref[...] = lax.dot_general(
-        taps_ref[...], grads_ref[...], (((0,), (0,)), ((), ())), preferred_element_type=F32
-    )
-    gg_ref[...] = gg_in[...]
-    loss_ref[0, 0] = loss_in[0, 0]
-
-
 def shards(tap_hidden, join_weight, norm_gain, head_weight, target_logits, seq_lengths, seq_mask):
     vmem = pl.BlockSpec(memory_space=pltpu.VMEM)
     smem = pl.BlockSpec(memory_space=pltpu.SMEM)
@@ -485,22 +507,7 @@
     scratch = list(shared_scratch().values())
     for rows in SPLITS:
         scratch += list(chain_scratch(rows).values())
-    loss, gain_grad, taps, grads = pl.pallas_call(
-        kernel,
-        out_shape=(
-            jax.ShapeDtypeStruct((1, 1), F32),
-            jax.ShapeDtypeStruct((8, COL), F32),
-            jax.ShapeDtypeStruct((TOK, TAPS * COL), BF16),
-            jax.ShapeDtypeStruct((TOK, LOC), BF16),
-        ),
-        in_specs=[hbm] * 7,
-        out_specs=(smem, vmem, vmem, vmem),
-        scratch_shapes=scratch,
-        compiler_params=pltpu.CompilerParams(
-            collective_id=0, has_side_effects=True, vmem_limit_bytes=60 * 1024 * 1024
-        ),
-        name="draft_step",
-    )(
+    inputs = (
         tap_hidden,
         join_weight.reshape(TAPS * COL, LOC),
         norm_gain.reshape(8, COL),
@@ -509,29 +516,21 @@
         seq_lengths,
         seq_mask,
     )
-    tile = 256
-    join_grad, gain_grad, loss = pl.pallas_call(
-        last_kernel,
-        grid=(LOC // tile,),
+    loss, gain_grad, join_grad = pl.pallas_call(
+        kernel,
         out_shape=(
+            jax.ShapeDtypeStruct((1, 1), F32),
+            jax.ShapeDtypeStruct((8, COL), F32),
             jax.ShapeDtypeStruct((TAPS * COL, LOC), F32),
-            jax.ShapeDtypeStruct((8, COL), F32),
-            jax.ShapeDtypeStruct((1, 1), F32),
         ),
-        in_specs=[
-            pl.BlockSpec((TOK, TAPS * COL), lambda i: (0, 0)),
-            pl.BlockSpec((TOK, tile), lambda i: (0, i)),
-            pl.BlockSpec((8, COL), lambda i: (0, 0)),
-            smem,
-        ],
-        out_specs=(
-            pl.BlockSpec((TAPS * COL, tile), lambda i: (0, i)),
-            pl.BlockSpec((8, COL), lambda i: (0, 0)),
-            smem,
+        in_specs=[hbm] * 7,
+        out_specs=(smem, vmem, vmem),
+        scratch_shapes=scratch,
+        compiler_params=pltpu.CompilerParams(
+            collective_id=0, has_side_effects=True, vmem_limit_bytes=40 * 1024 * 1024
         ),
-        compiler_params=pltpu.CompilerParams(vmem_limit_bytes=60 * 1024 * 1024),
-        name="join_gradient",
-    )(taps, grads, gain_grad, loss)
+        name="draft_step",
+    )(*[pltpu.with_memory_space_constraint(a, pltpu.HBM) for a in inputs])
     return loss.reshape(()), join_grad.reshape(TAPS, COL, LOC), gain_grad.reshape(LOC)
 
 

time: 110 us -> 107 us (0.973)
  Pallas kernels: 109 us -> 103 us
  local copies, waits for them, and re-layouts: 0 us -> 1.74 us
  between operations: 0.64 us -> 2.33 us
    pallas_call x1 -> x0, Pallas kernels: 4.7 us -> none  [shards(): pl.pallas_call(last_kernel, grid=(LOC // tile,), out_shape=(jax.ShapeDtyp...]
    unnamed x0 -> x2, local copies, waits for them, and re-layouts: none -> 1.74 us
    pallas_call x1, Pallas kernels: 105 us -> 103 us  [shards(): pl.pallas_call(kernel, out_shape=(jax.ShapeDtypeStruct((1, 1), F32), jax....]
where the time goes in v5:
time: 107 us
  Pallas kernels  103 us (96%)
  between operations  2.33 us (2%)
  local copies, waits for them, and re-layouts  1.74 us (2%)
    pallas_call x1, Pallas kernels, shards(): pl.pallas_call(kernel, out_shape=(jax.ShapeDtypeStruct((1, 1), F32), jax....  103 us

profile of v5, /device:TPU:1, one launch (start us, length us, event | category | flops | bytes accessed | tf_op | source)
XLA Modules:
  0.0 107.0 jit_solution(2259525724608253720)
XLA Ops:
  0.6 102.9 %draft_step.1 = (f32[1,1]{1,0:T(1,128)}, f32[8,128]{1,0:T(8,128)S(1)}, f32[384,1024]{1,0:T(8,128)S(1)}) custom-call(bf16[3,40,128]{2,1,0:T(8,128)(2,1)} %tap_hbm.1, bf16[384,1024]{1,0:T(8,128)(2,1)} %bitcast.7, f32[8,128]{1,0:T(8,128)} %bitcast.8, bf16[1024,1024]{1,0:T(8,128)(2,1)} %head_hbm.1, bf16[40,1024]{1,0:T(8,128)(2,1)} %tl_hbm.1, s32[10]{0:T(128)} %len_hbm.1, ...), custom_call_target="tpu_custom_call" | custom-call | tf_op jit(solution)/shard_map/draft_step/pallas_call | solution.py:519
  104.1 1.1 %copy.14 = f32[3,128,1024]{2,1,0:T(8,128)} copy(f32[3,128,1024]{2,1,0:T(8,128)S(1)} %bitcast.5) | data formatting | bytes 3145728
  105.2 0.6 copy.15

commit v6 on v5

--- a/solution.py
+++ b/solution.py
@@ -102,13 +102,17 @@
     return -(-tokens // 128) * 128
 
 
+def tap_rows(rows):
+    return -(-TAPS * rows // 16) * 16
+
+
 def chain_scratch(rows):
     V, dma = pltpu.VMEM, pltpu.SemaphoreType.DMA
     i32 = jnp.int32
     padded = pad128(8 * rows)
     half = LOC // 2
     buffers = dict(
-        tapl=V((8 * rows, TAPS * COL), BF16), tapt=V((TAPS * COL, padded), BF16), dfl=V((padded, LOC), BF16),
+        tapg=V((8, tap_rows(rows), COL), BF16), tapl=V((8 * rows, TAPS * COL), BF16), tapt=V((TAPS * COL, padded), BF16), dfl=V((padded, LOC), BF16),
         sb1=V((8, 4 * rows, COL), i32), rb1=V((8, 4 * rows, COL), i32),
         a1=V((8, rows, COL), F32), b1=V((8, rows, COL), F32), p1=V((rows, COL), F32), jy=V((8, rows, COL), F32),
         sqx=V((8, 1, padded), F32), sqb=V((8, 1, padded), F32), invc=V((8, rows, COL), F32),
@@ -121,9 +125,9 @@
         a2=V((8, rows, COL), F32), b2=V((8, rows, COL), F32), p2=V((rows, COL), F32), dn=V((8, rows, COL), F32),
         df=V((8, 8 * rows, COL), BF16),
     )
-    names = ("x1", "y1", "g1", "sx", "u", "sq", "s1", "s2", "x2", "y2", "g2", "df", "z", "zs", "c", "fw")
+    names = ("x1", "y1", "g1", "sx", "u", "sq", "s1", "s2", "x2", "y2", "g2", "df", "z", "zs", "c", "fw", "tf")
     sems = {side + name: dma for name in names for side in ("s_", "r_")}
-    sems.update(s_dl=dma, r_dl=dma((4,)))
+    sems.update(s_dl=dma, r_dl=dma((4,)), s_tap=dma, r_tap=dma((4,)))
     return buffers | sems
 
 
@@ -133,8 +137,8 @@
         tap=V((TAPS, BLK, COL), BF16), jw=V((TAPS * COL, LOC), BF16), gain=V((8, COL), F32),
         head=V((LOC, LOC), BF16), tl=V((BLK, LOC), BF16),
         len=pltpu.SMEM((SEQS,), jnp.int32), mask=pltpu.SMEM((SEQS,), jnp.int32),
-        tapg=V((8, 128, COL), BF16), ggb=V((8, 1, COL), F32), qb=V((8, 1, 128), F32),
-        s_in=dma((7,)), s_tap=dma, r_tap=dma((4,)), s_tf=dma, r_tf=dma, s_gg=dma, r_gg=dma, s_q=dma, r_q=dma,
+        ggb=V((8, 1, COL), F32), qb=V((8, 1, 128), F32),
+        s_in=dma((7,)), s_gg=dma, r_gg=dma, s_q=dma, r_q=dma,
     )
 
 
@@ -192,8 +196,13 @@
     for _, dev in sec_peers + xz_peers + y_peers:
         pl.semaphore_signal(barrier, inc=1, device_id=dev, device_id_type=MESH)
     loads[0].wait()
-    taps = [m.tap[k].astype(F32) for k in range(TAPS)] + [jnp.zeros((128 - TAPS * BLK, COL), F32)]
-    m.tapg[pi] = jnp.concatenate(taps, axis=0).astype(BF16)
+    taps = [m.tap[k].astype(F32) for k in range(TAPS)]
+    for i, rows in enumerate(SPLITS):
+        first = sum(SPLITS[:i])
+        parts = [tap[first : first + rows] for tap in taps]
+        if tap_rows(rows) > TAPS * rows:
+            parts.append(jnp.zeros((tap_rows(rows) - TAPS * rows, COL), F32))
+        chains[i].tapg[pi] = jnp.concatenate(parts, axis=0).astype(BF16)
     pl.semaphore_wait(barrier, 21)
 
     def copy_to(src, dst, s_sem, r_sem, dev):
@@ -232,10 +241,18 @@
         last.wait_recv()
         sent.append(last)
 
-    spread(m.tapg, m.s_tap, m.r_tap, m.s_tf, m.r_tf)
+    for w in chains:
+        spread(w.tapg, w.s_tap, w.r_tap, w.s_tf, w.r_tf)
     for load in loads[1:]:
         load.wait()
-    relay(m.tapg, m.s_tap, m.r_tap, m.s_tf, m.r_tf)
+
+    def send_two(tile, sb, rb, s_x, r_x):
+        for other in (2 * tile, 2 * tile + 1):
+            dev = (sec, lax.div(other, 4) * 32 + y * 4 + lax.rem(other, 4))
+
+            @pl.when(other != j)
+            def _():
+                copy_to(sb.at[other], rb.at[j], s_x, r_x, dev).start()
 
     def from_roots(rb):
         low, high = [root_value(half) for half in unpack(rb[0])]
@@ -251,7 +268,8 @@
         return total
 
     def vocab_sum(collect, rows, sb, rb, a_buf, b_buf, p_buf, out, s_x, r_x, s_y, r_y, s_g, r_g, between=None):
-        send_all(xz_peers, lambda other: sb.at[other], rb, s_x, r_x, j)
+        whole = rb.at[pl.ds(0, 7)]
+        sent.append(copy_to(whole, whole, s_x, r_x, xz_peers[0][1]))
         rb[j] = sb[j]
         if between is not None:
             between()
@@ -282,17 +300,19 @@
         half, tokens = 4 * rows, 8 * rows
         padded = pad128(tokens)
 
-        blocks = [m.tapg[p].astype(F32) for p in range(8)]
+        relay(w.tapg, w.s_tap, w.r_tap, w.s_tf, w.r_tf)
+        blocks = [w.tapg[p].astype(F32) for p in range(8)]
         for k in range(TAPS):
-            at = k * BLK + first
-            tap = jnp.concatenate([b[at : at + rows] for b in blocks], axis=0)
+            tap = jnp.concatenate([b[k * rows : (k + 1) * rows] for b in blocks], axis=0)
             w.tapl[:, k * COL : (k + 1) * COL] = tap.astype(BF16)
 
         def join_step(i, carry):
+            i = lax.rem(i + lax.div(j, 2) + 1, 4)
             at = pl.ds(pl.multiple_of(i * 256, 256), 256)
             acc = root_code(jnp.dot(w.tapl[...], m.jw[:, at], preferred_element_type=F32))
             w.sb1[2 * i] = pack(acc[:half, :COL], acc[half:, :COL])
             w.sb1[2 * i + 1] = pack(acc[:half, COL:], acc[half:, COL:])
+            send_two(i, w.sb1, w.rb1, w.s_x1, w.r_x1)
             return carry
 
         lax.fori_loop(0, 4, join_step, 0)
@@ -441,10 +461,12 @@
             w.dl[k * rows : (k + 2) * rows] = jnp.concatenate(pair, axis=0).astype(BF16)
 
         def grad_step(i, carry):
+            i = lax.rem(i + lax.div(j, 2) + 1, 4)
             at = pl.ds(pl.multiple_of(i * 256, 256), 256)
             acc = lax.dot_general(w.dl[...], m.head[at, :], (((1,), (1,)), ((), ())), preferred_element_type=F32)
             w.sb2[2 * i] = acc[:, :COL].astype(BF16)
             w.sb2[2 * i + 1] = acc[:, COL:].astype(BF16)
+            send_two(i, w.sb2, w.rb2, w.s_x2, w.r_x2)
             return carry
 
         lax.fori_loop(0, 4, grad_step, 0)

time: 107 us -> 107 us (level); the launches traced: 107 us -> 106 us
  Pallas kernels: 103 us -> 101 us
    pallas_call x1, Pallas kernels: 103 us -> 101 us  [shards(): pl.pallas_call(kernel, out_shape=(jax.ShapeDtypeStruct((1, 1), F32), jax....]
where the time goes in v6:
time: 107 us; the launch traced here: 106 us
  Pallas kernels  101 us (94%)
  between operations  2.33 us (2%)
  local copies, waits for them, and re-layouts  1.74 us (2%)
    pallas_call x1, Pallas kernels, shards(): pl.pallas_call(kernel, out_shape=(jax.ShapeDtypeStruct((1, 1), F32), jax....  101 us

profile of v6, /device:TPU:1, one launch (start us, length us, event | category | flops | bytes accessed | tf_op | source)
XLA Modules:
  0.0 105.5 jit_solution(16418762535400427282)
XLA Ops:
  0.6 101.4 %draft_step.1 = (f32[1,1]{1,0:T(1,128)}, f32[8,128]{1,0:T(8,128)S(1)}, f32[384,1024]{1,0:T(8,128)S(1)}) custom-call(bf16[3,40,128]{2,1,0:T(8,128)(2,1)} %tap_hbm.1, bf16[384,1024]{1,0:T(8,128)(2,1)} %bitcast.7, f32[8,128]{1,0:T(8,128)} %bitcast.8, bf16[1024,1024]{1,0:T(8,128)(2,1)} %head_hbm.1, bf16[40,1024]{1,0:T(8,128)(2,1)} %tl_hbm.1, s32[10]{0:T(128)} %len_hbm.1, ...), custom_call_target="tpu_custom_call" | custom-call | tf_op jit(solution)/shard_map/draft_step/pallas_call | solution.py:541
  102.6 1.1 %copy.14 = f32[3,128,1024]{2,1,0:T(8,128)} copy(f32[3,128,1024]{2,1,0:T(8,128)S(1)} %bitcast.5) | data formatting | bytes 3145728
  103.8 0.6 copy.15
